TPU v7x, 32 devices: a whole 2x2x4 slice. The times are simulated.
32 devices in a mesh: groups: 2 (over y), blk: 8 (over z, x), head: 2 (over core).
Axes of the slice: x: 2, y: 2, z: 4, core: 2. Of those that a mesh axis runs over, the one named last changes fastest.
Arguments:
- tokens: float32 [3072, 1024], P(('groups', 'blk'), 'head'), parts along dimension 0, may hold values from -20 to 20
- norm_gain: float32 [1024], replicated, may hold values from 0.1 to 1.9
- qkv_weight: bfloat16 [3, 1024, 1024], P(None, None, 'head'), may hold values from -20 to 20
- out_weight: bfloat16 [1024, 1024], P('head'), may hold values from -0.1875 to 0.1875
- lateral_weight: bfloat16 [2, 1024, 256], replicated, may hold values from -0.1875 to 0.1875
- conv_weight: bfloat16 [2, 3, 3, 256, 256], replicated, may hold values from -0.125 to 0.125
- level_gains: float32 [2, 2, 256], replicated, may hold values from 0.1 to 1.9
Outputs:
- fine_map: bfloat16 [32, 96, 256], P(('groups', 'blk'), 'head'), parts along dimension 0
- coarse_map: bfloat16 [16, 48, 256], P(('groups', 'blk'), 'head'), parts along dimension 0
There are 2 independent parts, one for each index of `groups`. A program takes and returns all parts, laid end to end along the dimension named above; an argument that names none is the same for every part. Nothing has to cross between parts.
All inputs are finite; a program needn't handle non-finite values.
Results may differ from a plain program's by a relative error of at most 0.014.
The roundings to bfloat16 on the way count: a program that leaves them out, or rounds other values in their place, can miss the bound.
Values may be sent and summed in bfloat16 or wider, within the bound.
A program may use at most 128 MiB of HBM per device.

v0:
```python
import math

import jax
import jax.numpy as jnp
from jax import lax
from jax.sharding import PartitionSpec as P

HEAD_DIM = 64
ROWS_DEV = 2
GW = 96


def padded_2(cells, sides, width):
    for axis, dim in sides:
        count = lax.axis_size(axis)
        ends = count - 1
        head = lax.slice_in_dim(cells, 0, width, axis=dim)
        tail = lax.slice_in_dim(cells, cells.shape[dim] - width, cells.shape[dim], axis=dim)
        cells = jnp.concatenate(
            [
                lax.ppermute(tail, axis, [(i, (i + 1) % count) for i in range(ends)]),
                cells,
                lax.ppermute(head, axis, [((i + 1) % count, i) for i in range(ends)]),
            ],
            axis=dim,
        )
    return cells


def layer_norm(values_in, gain_row):
    mean_row = jnp.mean(values_in, axis=-1, keepdims=True)
    centred = values_in - mean_row
    spread = jnp.mean(centred * centred, axis=-1, keepdims=True)
    return centred * lax.rsqrt(spread + 1e-06) * gain_row


def conv_taps(padded, kernel, row_count, col_count):
    total_out = jnp.zeros((row_count, col_count, kernel.shape[-1]), jnp.float32)
    for tap_row in range(3):
        for tap_col in range(3):
            window = padded[tap_row : tap_row + row_count, tap_col : tap_col + col_count]
            total_out = total_out + jnp.einsum(
                "rcd,de->rce", window, kernel[tap_row, tap_col], preferred_element_type=jnp.float32
            )
    return total_out


def lateral_norm(tile_in, lateral, gains):
    mixed = jnp.einsum("rcd,de->rce", tile_in, lateral, preferred_element_type=jnp.float32)
    return layer_norm(mixed, gains[0]).astype(jnp.bfloat16)


def make_attend(query_heads):
    tok_rows = query_heads.shape[0]
    heads_here = query_heads.shape[1]
    width_here = heads_here * HEAD_DIM
    score_scale = HEAD_DIM ** (-0.5)

    def attend_block(running_state, block_pair):
        running, totals, weighted = running_state
        key_block, value_block = block_pair
        key_count = key_block.shape[0]
        scores = (
            jnp.einsum(
                "qhd,khd->hqk",
                query_heads,
                key_block.reshape(key_count, heads_here, HEAD_DIM),
                preferred_element_type=jnp.float32,
            )
            * score_scale
        )
        newmax = jnp.maximum(running, jnp.max(scores, axis=-1))
        weights = jnp.exp(scores - newmax[:, :, None])
        factor = jnp.exp(running - newmax)
        totals = totals * factor + jnp.sum(weights, axis=-1)
        mixed_values = jnp.einsum(
            "hqk,khd->qhd",
            weights.astype(jnp.bfloat16),
            value_block.reshape(key_count, heads_here, HEAD_DIM),
            preferred_element_type=jnp.float32,
        )
        weighted = (
            weighted.reshape(tok_rows, heads_here, HEAD_DIM) * factor.T[:, :, None] + mixed_values
        )
        return ((newmax, totals, weighted.reshape(tok_rows, width_here)), None)

    def attend_piece(running_state, piece, start):
        key_piece, value_piece = piece
        key_count = key_piece.shape[0]
        block_rows = math.gcd(key_count, 1536)
        block_pairs = (
            key_piece.reshape(key_count // block_rows, block_rows, width_here),
            value_piece.reshape(key_count // block_rows, block_rows, width_here),
        )
        running_state, unused = lax.scan(attend_block, running_state, block_pairs)
        return running_state

    initial = (
        jnp.full((heads_here, tok_rows), -jnp.inf, jnp.float32),
        jnp.zeros((heads_here, tok_rows), jnp.float32),
        jnp.zeros((tok_rows, width_here), jnp.float32),
    )
    return (attend_piece, initial)


def finish_state(final_state):
    running, totals, weighted = final_state
    heads_here = totals.shape[0]
    tok_rows = totals.shape[1]
    return (
        (weighted.reshape(tok_rows, heads_here, HEAD_DIM) / totals.T[:, :, None])
        .reshape(tok_rows, heads_here * HEAD_DIM)
        .astype(jnp.bfloat16)
    )


def body(tokens, norm_gain, qkv_weight, out_weight, lateral_weight, conv_weight, level_gains):
    gathered = lax.all_gather(tokens, "head", axis=1, tiled=True)
    normed = layer_norm(gathered, norm_gain).astype(jnp.bfloat16)
    queries = jnp.dot(normed, qkv_weight[0], preferred_element_type=jnp.float32).astype(
        jnp.bfloat16
    )
    key_rows = jnp.dot(normed, qkv_weight[1], preferred_element_type=jnp.float32).astype(
        jnp.bfloat16
    )
    value_rows = jnp.dot(normed, qkv_weight[2], preferred_element_type=jnp.float32).astype(
        jnp.bfloat16
    )
    tok_rows = queries.shape[0]
    width_dev = queries.shape[1]
    heads_dev = width_dev // HEAD_DIM
    blk_count = lax.axis_size("blk")
    slices = blk_count // heads_dev
    slice_rows = tok_rows // slices
    query_send = jnp.transpose(
        queries.reshape(slices, slice_rows, heads_dev, HEAD_DIM), (2, 0, 1, 3)
    ).reshape(blk_count, slice_rows * HEAD_DIM)
    pair_heads = jnp.concatenate(
        (
            key_rows.reshape(tok_rows, heads_dev, HEAD_DIM),
            value_rows.reshape(tok_rows, heads_dev, HEAD_DIM),
        ),
        axis=2,
    )
    pair_heads = jnp.transpose(pair_heads, (1, 0, 2))
    pair_send = jnp.broadcast_to(
        pair_heads[:, None], (heads_dev, slices, tok_rows, 2 * HEAD_DIM)
    ).reshape(blk_count, tok_rows, 2 * HEAD_DIM)
    query_moved, pair_moved = (
        lax.all_to_all(query_send, "blk", split_axis=0, concat_axis=0, tiled=True),
        lax.all_to_all(pair_send, "blk", split_axis=0, concat_axis=0, tiled=True),
    )
    query_count = blk_count * slice_rows
    pair_whole = pair_moved.reshape(blk_count * tok_rows, 2 * HEAD_DIM)
    attend_piece, initial = make_attend(query_moved.reshape(query_count, 1, HEAD_DIM))
    one_head = finish_state(
        attend_piece(initial, (pair_whole[:, :HEAD_DIM], pair_whole[:, HEAD_DIM:]), 0)
    )
    returned = lax.all_to_all(
        one_head.reshape(blk_count, slice_rows * HEAD_DIM),
        "blk",
        split_axis=0,
        concat_axis=0,
        tiled=True,
    )
    attended = jnp.transpose(
        returned.reshape(heads_dev, slices, slice_rows, HEAD_DIM), (1, 2, 0, 3)
    ).reshape(tok_rows, width_dev)
    col_width = GW // lax.axis_size("head")
    partial_value = jnp.dot(attended, out_weight, preferred_element_type=jnp.float32).reshape(
        ROWS_DEV, GW, -1
    )
    branch = lax.psum_scatter(
        partial_value.astype(jnp.bfloat16), "head", scatter_dimension=1, tiled=True
    ).astype(jnp.float32)
    residual = lax.dynamic_slice_in_dim(
        gathered.reshape(ROWS_DEV, GW, -1), lax.axis_index("head") * col_width, col_width, 1
    )
    block_out = (residual + branch).astype(jnp.bfloat16)
    fine_in = lateral_norm(block_out, lateral_weight[0], level_gains[0])
    fine_pad = padded_2(fine_in, (("blk", 0), ("head", 1)), 1)
    fine_level = layer_norm(
        conv_taps(fine_pad, conv_weight[0], ROWS_DEV, col_width), level_gains[0, 1]
    ).astype(jnp.bfloat16)
    pooled = jnp.max(block_out.reshape(ROWS_DEV // 2, 2, col_width // 2, 2, -1), axis=(1, 3))
    coarse_in = lateral_norm(pooled, lateral_weight[1], level_gains[1])
    coarse_pad = padded_2(coarse_in, (("blk", 0), ("head", 1)), 1)
    coarse_level = layer_norm(
        conv_taps(coarse_pad, conv_weight[1], ROWS_DEV // 2, col_width // 2), level_gains[1, 1]
    ).astype(jnp.bfloat16)
    return (fine_level, coarse_level)


def solution(mesh):
    in_specs = (
        P(("groups", "blk"), "head"),
        P(),
        P(None, None, "head"),
        P("head", None),
        P(),
        P(),
        P(),
    )
    out_specs = (P(("groups", "blk"), "head", None), P(("groups", "blk"), "head", None))
    return jax.shard_map(body, mesh=mesh, in_specs=in_specs, out_specs=out_specs, check_vma=False)
```

profile of v0, /device:TPU:9, one launch (start us, length us, event | category | flops | bytes accessed | tf_op | source)
XLA Modules:
  0.0 112.4 jit_solution(10356113668897213138)
XLA Ops:
  7.2 3.0 %all_gather.3 = f32[192,1024]{1,0:T(8,128)S(1)} all-gather(f32[192,512]{1,0:T(8,128)} %param.7), channel_id=1, replica_groups=mesh['groups'=2,'blk'=8,'head'=2] {'head'}, dimensions={1}, use_global_device_ids=true | all-gather | bytes 1179648 | tf_op jit(solution)/shard_map/all_gather | solution.py:118
  10.3 0.2 multiply_reduce_fusion
  10.8 1.6 %convolution_convert_fusion.3 = bf16[192,512]{1,0:T(8,128)(2,1)S(1)} fusion(bf16[192,1024]{1,0:T(8,128)(2,1)S(1)} %multiply_convert_fusion, bf16[3,1024,512]{2,1,0:T(8,128)(2,1)} %param.9), kind=kOutput, calls=%fused_computation.16 | convolution fusion | flops 201424896 | bytes 1638400 | tf_op jit(solution)/shard_map/dot_general | solution.py:120
  12.5 0.2 copy.38
  13.0 0.5 broadcast.179
  13.5 1.8 %reduce.17 = bf16[8,12288]{1,0:T(8,128)(2,1)S(1)} reduce(bf16[8,1,12288]{2,1,0:T(2,128)(2,1)S(1)} %all_to_all.17, bf16[]{:T(256)} %broadcast.179), dimensions={1}, to_apply=%all_to_all.17.reduce_sub_computation | reduce | bytes 393218 | tf_op jit(solution)/shard_map/all_to_all | solution.py:150
  15.3 0.8 reshape.309
  16.1 5.7 %all-to-all-start = ((bf16[8,2,6144]{2,1,0:T(2,128)(2,1)}), bf16[8,2,6144]{2,1,0:T(2,128)(2,1)S(1)}, u32[]{:S(2)}, u32[]{:S(2)}) async-start(bf16[8,2,6144]{2,1,0:T(2,128)(2,1)} %reshape.309), calls=%async_computation | async-start | bytes 393216 | tf_op jit(solution)/shard_map/all_to_all | solution.py:150
  21.8 1.6 %convolution_convert_fusion.2 = bf16[192,512]{1,0:T(8,128)(2,1)S(1)} fusion(bf16[192,1024]{1,0:T(8,128)(2,1)S(1)} %multiply_convert_fusion, bf16[3,1024,512]{2,1,0:T(8,128)(2,1)} %param.9), kind=kOutput, calls=%fused_computation.15 | convolution fusion | flops 201424896 | bytes 1638400 | tf_op jit(solution)/shard_map/dot_general | solution.py:123
  23.5 1.6 %convolution_convert_fusion.1 = bf16[192,512]{1,0:T(8,128)(2,1)S(1)} fusion(bf16[192,1024]{1,0:T(8,128)(2,1)S(1)} %multiply_convert_fusion, bf16[3,1024,512]{2,1,0:T(8,128)(2,1)} %param.9), kind=kOutput, calls=%fused_computation.14 | convolution fusion | flops 201424896 | bytes 1638400 | tf_op jit(solution)/shard_map/dot_general | solution.py:126
  25.4 0.9 copy.42
  26.3 1.0 all-to-all-done
  27.4 5.3 %all-to-all-start.1 = ((bf16[8,192,128]{2,1,0:T(8,128)(2,1)}), bf16[8,192,128]{2,1,0:T(8,128)(2,1)S(1)}, u32[]{:S(2)}, u32[]{:S(2)}) async-start(bf16[8,192,128]{2,1,0:T(8,128)(2,1)} %copy.42), calls=%async_computation.1 | async-start | bytes 786432 | tf_op jit(solution)/shard_map/all_to_all | solution.py:151
  32.8 1.2 %reduce.15 = bf16[8,12288]{1,0:T(8,128)(2,1)S(1)} reduce(bf16[8,1,12288]{2,1,0:T(2,128)(2,1)S(1)} %reshape.310, bf16[]{:T(256)} %constant.51), dimensions={1}, to_apply=%all_to_all.14.reduce_sub_computation | reduce | bytes 393218 | tf_op jit(solution)/shard_map/all_to_all | solution.py:150
  34.0 0.4 reshape.279
  34.4 6.3 %all-to-all-done.1 = bf16[8,192,128]{2,1,0:T(8,128)(2,1)S(1)} async-done(((bf16[8,192,128]{2,1,0:T(8,128)(2,1)}), bf16[8,192,128]{2,1,0:T(8,128)(2,1)S(1)}, u32[]{:S(2)}, u32[]{:S(2)}) %all-to-all-start.1) | async-done | bytes 393248 | tf_op jit(solution)/shard_map/all_to_all | solution.py:151
  40.7 1.4 %fusion.119 = (f32[1536]{0:T(1024)S(1)}, f32[1536,1536]{0,1:T(8,128)S(1)}) fusion(bf16[1536,64]{1,0:T(8,128)(2,1)S(1)} %reshape.279, bf16[1536,128]{1,0:T(8,128)(2,1)S(1)} %bitcast.176), kind=kOutput, calls=%fused_computation.177 | convolution fusion | flops 306706944 | bytes 10033152 | tf_op jit(solution)/shard_map/while/body/eval_jaxpr/qhd,khd->hqk/dot_general | solution.py:64
  42.1 1.3 %fusion = f32[1536]{0:T(1024)S(1)} fusion(f32[1536,1536]{0,1:T(8,128)S(1)} %get-tuple-element.42, f32[1536]{0:T(1024)S(1)} %get-tuple-element.41), kind=kLoop, calls=%fused_computation.2 | loop fusion | flops 4717056 | bytes 9449472 | tf_op jit(solution)/shard_map/while/body/eval_jaxpr/reduce_sum | solution.py:75
  43.4 1.6 %fusion.17 = bf16[1536,1,64]{0,2,1:T(8,128)(2,1)S(1)} fusion(f32[1536,1536]{0,1:T(8,128)S(1)} %get-tuple-element.42, f32[1536]{0:T(1024)S(1)} %get-tuple-element.41, bf16[1536,128]{1,0:T(8,128)(2,1)S(1)} %bitcast.177, f32[1536]{0:T(1024)S(1)} %get-tuple-element.36, f32[1536]{0:T(1024)S(1)} %get-tuple-element.35), kind=kOutput, calls=%fused_computation.10 | convolution fusion | flops 307003392 | bytes 10045440 | tf_op jit(solution)/shard_map/while/body/eval_jaxpr/hqk,khd->qhd/dot_general | solution.py:76
  45.0 0.2 copy.43
  45.3 0.2 convert_element_type.78
  45.5 1.8 %reduce.18 = bf16[8,12288]{1,0:T(8,128)(2,1)S(1)} reduce(bf16[8,1,12288]{2,1,0:T(2,128)(2,1)S(1)} %convert_element_type.78, bf16[]{:T(256)} %broadcast.179), dimensions={1}, to_apply=%convert_element_type.78.reduce_sub_computation | reduce | bytes 393218 | tf_op jit(solution)/shard_map/convert_element_type | solution.py:113
  47.4 11.4 %all_to_all.21 = bf16[8,2,6144]{2,1,0:T(2,128)(2,1)S(1)} all-to-all(bf16[8,2,6144]{2,1,0:T(2,128)(2,1)S(1)} %reshape.311), channel_id=1, replica_groups=mesh['groups'=2,'blk'=8,'head'=2] {'blk'}, dimensions={0} | all-to-all | bytes 393216 | tf_op jit(solution)/shard_map/all_to_all | solution.py:159
  59.0 1.2 %reduce.16 = bf16[8,12288]{1,0:T(8,128)(2,1)S(1)} reduce(bf16[8,1,12288]{2,1,0:T(2,128)(2,1)S(1)} %reshape.312, bf16[]{:T(256)} %constant.51), dimensions={1}, to_apply=%all_to_all.16.reduce_sub_computation | reduce | bytes 393218 | tf_op jit(solution)/shard_map/all_to_all | solution.py:159
  60.2 0.4 reshape.283
  60.6 0.3 copy.48
  60.9 0.3 reshape.303
  61.1 1.2 %convolution_convert_fusion = bf16[2,96,1024]{2,1,0:T(8,128)(2,1)} fusion(bf16[2,96,512]{2,1,0:T(8,128)(2,1)S(1)} %reshape.303, bf16[512,1024]{1,0:T(8,128)(2,1)S(1)} %copy-done), kind=kOutput, calls=%fused_computation.11 | convolution fusion | flops 201523200 | bytes 1638400 | tf_op jit(solution)/shard_map/dot_general | solution.py:170
  62.3 2.8 %slice_bitcast_fusion = (bf16[3,3,256,256]{3,2,1,0:T(8,128)(2,1)}, bf16[3,3,256,256]{3,2,1,0:T(8,128)(2,1)S(1)}) fusion(bf16[2,3,3,256,256]{4,3,2,1,0:T(8,128)(2,1)} %param.12), kind=kLoop, calls=%fused_computation.12 | loop fusion | bytes 4718592 | tf_op jit(solution)/shard_map/squeeze | solution.py:189
  65.2 7.5 %reduce-scatter.2.cloned.1.call-done = bf16[2,48,1024]{2,1,0:T(8,128)(2,1)} async-done(((bf16[2,96,1024]{2,1,0:T(8,128)(2,1)}), bf16[2,48,1024]{2,1,0:T(8,128)(2,1)}) %reduce-scatter.2.cloned.1.call-update) | async-done | bytes 196624 | tf_op jit(solution)/shard_map/reduce_scatter | solution.py:173
  72.7 1.0 fusion.116
  73.7 0.2 reduce_max.29
  74.0 1.4 %fusion.122 = (f32[24]{0:T(128)S(1)}, f32[24,256]{1,0:T(8,128)S(1)}) fusion(bf16[24,1024]{1,0:T(8,128)(2,1)S(1)} %reduce_max.29, bf16[2,1024,256]{2,1,0:T(8,128)(2,1)} %param.11), kind=kOutput, calls=%fused_computation.180 | convolution fusion | flops 12589032 | bytes 598112 | tf_op jit(solution)/shard_map/rcd,de->rce/dot_general | solution.py:49
  75.7 3.1 %collective-permute-start.4 = (bf16[1,24,256]{2,1,0:T(8,128)(2,1)S(1)}, bf16[1,24,256]{2,1,0:T(8,128)(2,1)S(1)}, u32[]{:S(2)}, u32[]{:S(2)}) collective-permute-start(bf16[1,24,256]{2,1,0:T(8,128)(2,1)S(1)} %fusion.115), channel_id=1, source_target_pairs={{0,2},{2,4},{4,6},{6,8},{8,10},{10,12},{12,14},{1,3},{3,5},{5,7},{... | collective-permute-start | bytes 36872 | tf_op jit(solution)/shard_map/ppermute | solution.py:21
  78.8 3.1 %collective-permute-start.5 = (bf16[1,24,256]{2,1,0:T(8,128)(2,1)S(1)}, bf16[1,24,256]{2,1,0:T(8,128)(2,1)S(1)}, u32[]{:S(2)}, u32[]{:S(2)}) collective-permute-start(bf16[1,24,256]{2,1,0:T(8,128)(2,1)S(1)} %fusion.115), channel_id=1, source_target_pairs={{2,0},{4,2},{6,4},{8,6},{10,8},{12,10},{14,12},{3,1},{5,3},{7,5},{... | collective-permute-start | bytes 36872 | tf_op jit(solution)/shard_map/ppermute | solution.py:23
  81.9 1.3 %fusion.120 = (f32[2,48]{1,0:T(2,128)S(1)}, f32[2,48,256]{2,1,0:T(8,128)S(1)}) fusion(bf16[2,48,1024]{2,1,0:T(8,128)(2,1)S(1)} %get-tuple-element.17, bf16[2,1024,256]{2,1,0:T(8,128)(2,1)} %param.11), kind=kOutput, calls=%fused_computation.178 | convolution fusion | flops 50356128 | bytes 819584 | tf_op jit(solution)/shard_map/rcd,de->rce/dot_general | solution.py:49
  83.6 2.2 %collective-permute-start = (bf16[1,48,256]{2,1,0:T(8,128)(2,1)S(1)}, bf16[1,48,256]{2,1,0:T(8,128)(2,1)S(1)}, u32[]{:S(2)}, u32[]{:S(2)}) collective-permute-start(bf16[1,48,256]{2,1,0:T(8,128)(2,1)S(1)} %get-tuple-element.31), channel_id=1, source_target_pairs={{0,2},{2,4},{4,6},{6,8},{8,10},{10,12},{12,14},{1,3},{3,5},{5,7},{... | collective-permute-start | bytes 73736 | tf_op jit(solution)/shard_map/ppermute | solution.py:21
  85.8 4.0 %collective-permute-start.1 = (bf16[1,48,256]{2,1,0:T(8,128)(2,1)S(1)}, bf16[1,48,256]{2,1,0:T(8,128)(2,1)S(1)}, u32[]{:S(2)}, u32[]{:S(2)}) collective-permute-start(bf16[1,48,256]{2,1,0:T(8,128)(2,1)S(1)} %get-tuple-element.32), channel_id=1, source_target_pairs={{2,0},{4,2},{6,4},{8,6},{10,8},{12,10},{14,12},{3,1},{5,3},{7,5},{... | collective-permute-start | bytes 73736 | tf_op jit(solution)/shard_map/ppermute | solution.py:23
  90.1 3.2 %collective-permute-start.7 = (bf16[3,1,256]{2,1,0:T(2,128)(2,1)S(1)}, bf16[3,1,256]{2,1,0:T(2,128)(2,1)S(1)}, u32[]{:S(2)}, u32[]{:S(2)}) collective-permute-start(bf16[3,1,256]{2,1,0:T(2,128)(2,1)S(1)} %get-tuple-element.34), channel_id=1, source_target_pairs={{1,0},{3,2},{5,4},{7,6},{9,8},{11,10},{13,12},{15,14},{17,16},{19,... | collective-permute-start | bytes 4616 | tf_op jit(solution)/shard_map/ppermute | solution.py:23
  93.3 1.3 %collective-permute-start.6 = (bf16[3,1,256]{2,1,0:T(2,128)(2,1)S(1)}, bf16[3,1,256]{2,1,0:T(2,128)(2,1)S(1)}, u32[]{:S(2)}, u32[]{:S(2)}) collective-permute-start(bf16[3,1,256]{2,1,0:T(2,128)(2,1)S(1)} %get-tuple-element.33), channel_id=1, source_target_pairs={{0,1},{2,3},{4,5},{6,7},{8,9},{10,11},{12,13},{14,15},{16,17},{18,... | collective-permute-start | bytes 4616 | tf_op jit(solution)/shard_map/ppermute | solution.py:21
  94.9 1.5 %collective-permute-done.6 = bf16[3,1,256]{2,1,0:T(2,128)(2,1)S(1)} collective-permute-done((bf16[3,1,256]{2,1,0:T(2,128)(2,1)S(1)}, bf16[3,1,256]{2,1,0:T(2,128)(2,1)S(1)}, u32[]{:S(2)}, u32[]{:S(2)}) %collective-permute-start.6) | collective-permute-done | bytes 1568 | tf_op jit(solution)/shard_map/ppermute | solution.py:21
  97.2 0.3 fusion.123
  97.6 0.7 fusion.73
  98.4 1.3 %collective-permute-start.2 = (bf16[4,1,256]{2,1,0:T(2,128)(2,1)S(1)}, bf16[4,1,256]{2,1,0:T(2,128)(2,1)S(1)}, u32[]{:S(2)}, u32[]{:S(2)}) collective-permute-start(bf16[4,1,256]{2,1,0:T(2,128)(2,1)S(1)} %get-tuple-element.29), channel_id=1, source_target_pairs={{0,1},{2,3},{4,5},{6,7},{8,9},{10,11},{12,13},{14,15},{16,17},{18,... | collective-permute-start | bytes 6152 | tf_op jit(solution)/shard_map/ppermute | solution.py:21
  99.7 3.0 %collective-permute-start.3 = (bf16[4,1,256]{2,1,0:T(2,128)(2,1)S(1)}, bf16[4,1,256]{2,1,0:T(2,128)(2,1)S(1)}, u32[]{:S(2)}, u32[]{:S(2)}) collective-permute-start(bf16[4,1,256]{2,1,0:T(2,128)(2,1)S(1)} %get-tuple-element.30), channel_id=1, source_target_pairs={{1,0},{3,2},{5,4},{7,6},{9,8},{11,10},{13,12},{15,14},{17,16},{19,... | collective-permute-start | bytes 6152 | tf_op jit(solution)/shard_map/ppermute | solution.py:23
  103.0 0.5 collective-permute-done.3
  104.3 0.2 fusion.121
  104.8 0.7 multiply_convert_fusion.1
  (65 shorter events, 5.1 us)
Async XLA Ops:
  7.2 54.0 %copy-start = (bf16[512,1024]{1,0:T(8,128)(2,1)S(1)}, bf16[512,1024]{1,0:T(8,128)(2,1)}, u32[]{:S(2)}) copy-start(bf16[512,1024]{1,0:T(8,128)(2,1)} %param.10) | copy-start | bytes 3145732
  7.2 3.4 %copy-start.2 = (f32[1024]{0:T(1024)S(1)}, f32[1024]{0:T(1024)}, u32[]{:S(2)}) copy-start(f32[1024]{0:T(1024)} %param.8) | copy-start | bytes 12292
  16.1 11.3 %all-to-all-start = ((bf16[8,2,6144]{2,1,0:T(2,128)(2,1)}), bf16[8,2,6144]{2,1,0:T(2,128)(2,1)S(1)}, u32[]{:S(2)}, u32[]{:S(2)}) async-start(bf16[8,2,6144]{2,1,0:T(2,128)(2,1)} %reshape.309), calls=%async_computation | async-start | bytes 393216 | tf_op jit(solution)/shard_map/all_to_all | solution.py:150
  27.4 13.3 %all-to-all-start.1 = ((bf16[8,192,128]{2,1,0:T(8,128)(2,1)}), bf16[8,192,128]{2,1,0:T(8,128)(2,1)S(1)}, u32[]{:S(2)}, u32[]{:S(2)}) async-start(bf16[8,192,128]{2,1,0:T(8,128)(2,1)} %copy.42), calls=%async_computation.1 | async-start | bytes 786432 | tf_op jit(solution)/shard_map/all_to_all | solution.py:151
  32.6 40.0 %reduce-scatter.2.cloned.1.call-start = ((), (), s32[]{:S(2)}) async-start(), calls=%async_computation.4 | async-start | bytes 589824 | tf_op jit(solution)/shard_map/reduce_scatter | solution.py:173
  60.8 1.5 %copy-start.3 = (f32[2,2,256]{2,1,0:T(2,128)S(1)}, f32[2,2,256]{2,1,0:T(2,128)}, u32[]{:S(2)}) copy-start(f32[2,2,256]{2,1,0:T(2,128)} %param.13) | copy-start | bytes 12292
  74.0 15.9 %copy-start.1 = (bf16[3,3,256,256]{3,2,1,0:T(8,128)(2,1)S(1)}, bf16[3,3,256,256]{3,2,1,0:T(8,128)(2,1)}, u32[]{:S(2)}) copy-start(bf16[3,3,256,256]{3,2,1,0:T(8,128)(2,1)} %get-tuple-element.18) | copy-start | bytes 3538948
  75.7 14.4 %collective-permute-start.4 = (bf16[1,24,256]{2,1,0:T(8,128)(2,1)S(1)}, bf16[1,24,256]{2,1,0:T(8,128)(2,1)S(1)}, u32[]{:S(2)}, u32[]{:S(2)}) collective-permute-start(bf16[1,24,256]{2,1,0:T(8,128)(2,1)S(1)} %fusion.115), channel_id=1, source_target_pairs={{0,2},{2,4},{4,6},{6,8},{8,10},{10,12},{12,14},{1,3},{3,5},{5,7},{... | collective-permute-start | bytes 36872 | tf_op jit(solution)/shard_map/ppermute | solution.py:21
  78.8 11.3 %collective-permute-start.5 = (bf16[1,24,256]{2,1,0:T(8,128)(2,1)S(1)}, bf16[1,24,256]{2,1,0:T(8,128)(2,1)S(1)}, u32[]{:S(2)}, u32[]{:S(2)}) collective-permute-start(bf16[1,24,256]{2,1,0:T(8,128)(2,1)S(1)} %fusion.115), channel_id=1, source_target_pairs={{2,0},{4,2},{6,4},{8,6},{10,8},{12,10},{14,12},{3,1},{5,3},{7,5},{... | collective-permute-start | bytes 36872 | tf_op jit(solution)/shard_map/ppermute | solution.py:23
  83.6 14.8 %collective-permute-start = (bf16[1,48,256]{2,1,0:T(8,128)(2,1)S(1)}, bf16[1,48,256]{2,1,0:T(8,128)(2,1)S(1)}, u32[]{:S(2)}, u32[]{:S(2)}) collective-permute-start(bf16[1,48,256]{2,1,0:T(8,128)(2,1)S(1)} %get-tuple-element.31), channel_id=1, source_target_pairs={{0,2},{2,4},{4,6},{6,8},{8,10},{10,12},{12,14},{1,3},{3,5},{5,7},{... | collective-permute-start | bytes 73736 | tf_op jit(solution)/shard_map/ppermute | solution.py:21
  85.8 12.6 %collective-permute-start.1 = (bf16[1,48,256]{2,1,0:T(8,128)(2,1)S(1)}, bf16[1,48,256]{2,1,0:T(8,128)(2,1)S(1)}, u32[]{:S(2)}, u32[]{:S(2)}) collective-permute-start(bf16[1,48,256]{2,1,0:T(8,128)(2,1)S(1)} %get-tuple-element.32), channel_id=1, source_target_pairs={{2,0},{4,2},{6,4},{8,6},{10,8},{12,10},{14,12},{3,1},{5,3},{7,5},{... | collective-permute-start | bytes 73736 | tf_op jit(solution)/shard_map/ppermute | solution.py:23
  90.1 6.6 %collective-permute-start.7 = (bf16[3,1,256]{2,1,0:T(2,128)(2,1)S(1)}, bf16[3,1,256]{2,1,0:T(2,128)(2,1)S(1)}, u32[]{:S(2)}, u32[]{:S(2)}) collective-permute-start(bf16[3,1,256]{2,1,0:T(2,128)(2,1)S(1)} %get-tuple-element.34), channel_id=1, source_target_pairs={{1,0},{3,2},{5,4},{7,6},{9,8},{11,10},{13,12},{15,14},{17,16},{19,... | collective-permute-start | bytes 4616 | tf_op jit(solution)/shard_map/ppermute | solution.py:23
  93.3 3.1 %collective-permute-start.6 = (bf16[3,1,256]{2,1,0:T(2,128)(2,1)S(1)}, bf16[3,1,256]{2,1,0:T(2,128)(2,1)S(1)}, u32[]{:S(2)}, u32[]{:S(2)}) collective-permute-start(bf16[3,1,256]{2,1,0:T(2,128)(2,1)S(1)} %get-tuple-element.33), channel_id=1, source_target_pairs={{0,1},{2,3},{4,5},{6,7},{8,9},{10,11},{12,13},{14,15},{16,17},{18,... | collective-permute-start | bytes 4616 | tf_op jit(solution)/shard_map/ppermute | solution.py:21
  98.4 4.7 %collective-permute-start.2 = (bf16[4,1,256]{2,1,0:T(2,128)(2,1)S(1)}, bf16[4,1,256]{2,1,0:T(2,128)(2,1)S(1)}, u32[]{:S(2)}, u32[]{:S(2)}) collective-permute-start(bf16[4,1,256]{2,1,0:T(2,128)(2,1)S(1)} %get-tuple-element.29), channel_id=1, source_target_pairs={{0,1},{2,3},{4,5},{6,7},{8,9},{10,11},{12,13},{14,15},{16,17},{18,... | collective-permute-start | bytes 6152 | tf_op jit(solution)/shard_map/ppermute | solution.py:21
  99.7 3.8 %collective-permute-start.3 = (bf16[4,1,256]{2,1,0:T(2,128)(2,1)S(1)}, bf16[4,1,256]{2,1,0:T(2,128)(2,1)S(1)}, u32[]{:S(2)}, u32[]{:S(2)}) collective-permute-start(bf16[4,1,256]{2,1,0:T(2,128)(2,1)S(1)} %get-tuple-element.30), channel_id=1, source_target_pairs={{1,0},{3,2},{5,4},{7,6},{9,8},{11,10},{13,12},{15,14},{17,16},{19,... | collective-permute-start | bytes 6152 | tf_op jit(solution)/shard_map/ppermute | solution.py:23
Sparse Core Ops, SparseCore 0:
  62.4 10.1 reduce-scatter.1
where the time goes:
time: 113 us; the launch traced here: 112 us
  starting transfers between devices  32.1 us (28%)
  waiting for transfers between devices  16.8 us (15%)
  matrix products  14.7 us (13%)
  between operations  14.5 us (13%)
  blocking collectives  14.4 us (13%)
  other arithmetic  11.5 us (10%)
  local copies, waits for them, and re-layouts  8.16 us (7%)
    ppermute x4, starting transfers between devices, padded_2(): lax.ppermute(head, axis, [((i + 1) % count, i) for i in range(ends)])  13.3 us
    all_to_all x1, blocking collectives, body(): lax.all_to_all(one_head.reshape(blk_count, slice_rows * HEAD_DIM), 'blk',...  11.4 us
    ppermute x4, starting transfers between devices, padded_2(): lax.ppermute(tail, axis, [(i, (i + 1) % count) for i in range(ends)])  7.85 us
    reduce_scatter x1, waiting for transfers between devices, body(): lax.psum_scatter(partial_value.astype(jnp.bfloat16), 'head', scatter_dime...  7.51 us
    all_to_all x1, waiting for transfers between devices, body(): lax.all_to_all(pair_send, 'blk', split_axis=0, concat_axis=0, tiled=True)  6.29 us
    all_to_all x1, starting transfers between devices, body(): lax.all_to_all(query_send, 'blk', split_axis=0, concat_axis=0, tiled=True)  5.69 us
    all_to_all x1, starting transfers between devices, body(): lax.all_to_all(pair_send, 'blk', split_axis=0, concat_axis=0, tiled=True)  5.28 us
    all_gather x1, blocking collectives, body(): gathered = lax.all_gather(tokens, 'head', axis=1, tiled=True)  3.01 us
  transfers between devices with their start and end apart: 11, of which 5 were waited for; matrix products, arithmetic and copies ran while one was open for 12% of the time, Pallas kernels for 0%

commit v1 on v0

v1 whole, which is shorter than its diff:
```python
import functools

import jax
import jax.numpy as jnp
from jax import lax
from jax.experimental import pallas as pl
from jax.experimental.pallas import tpu as pltpu
from jax.sharding import PartitionSpec as P

HEAD_DIM = 64
ROWS_DEV = 2
GW = 96
SUBS = 2
F32 = jnp.float32
BF16 = jnp.bfloat16
NT = (((1,), (1,)), ((), ()))


def layer_norm(values_in, gain_row):
    mean_row = jnp.mean(values_in, axis=-1, keepdims=True)
    centred = values_in - mean_row
    spread = jnp.mean(centred * centred, axis=-1, keepdims=True)
    return centred * lax.rsqrt(spread + 1e-06) * gain_row


def dot(lhs, rhs):
    return jnp.dot(lhs, rhs, preferred_element_type=F32)


def dot_nt(lhs, rhs):
    return lax.dot_general(lhs, rhs, NT, preferred_element_type=F32)


def kernel(
    count,
    tokens_ref, gain_ref, qkv_hbm, out_hbm, lateral_hbm, conv_hbm, gains_ref,
    fine_ref, coarse_ref,
    tok, qkv, out_w, lat_w, conv_w, wvt, normed, ring, other, qbd, kbuf, vbuf,
    acc, peak, total, att, part_send, part_recv, fpad, cpad, fcol, ccol,
    load_sem, tok_sem, ring_send, ring_recv, sib_send, sib_recv, part_sem, halo_send, halo_recv,
):
    blk = lax.axis_index("blk")
    head = lax.axis_index("head")
    sib = 1 - head
    rows = tok.shape[1]
    half = rows // 2
    cols = GW // 2
    pairs = qbd.shape[0]
    pair_rows = qbd.shape[1]

    even = blk % 2 == 0
    up_ring = jnp.where(
        even, jnp.where(blk == count - 2, blk + 1, blk + 2), jnp.where(blk == 1, blk - 1, blk - 2)
    )
    down_ring = jnp.where(
        even, jnp.where(blk == 0, blk + 1, blk - 2), jnp.where(blk == count - 1, blk - 1, blk + 2)
    )
    target = jnp.where(head == 0, up_ring, down_ring)
    source = jnp.where(head == 0, down_ring, up_ring)

    loads = [
        pltpu.make_async_copy(tokens_ref, tok.at[head], load_sem.at[0]),
        pltpu.make_async_copy(qkv_hbm.at[2], qkv.at[2], load_sem.at[1]),
        pltpu.make_async_copy(qkv_hbm.at[0], qkv.at[0], load_sem.at[2]),
        pltpu.make_async_copy(qkv_hbm.at[1], qkv.at[1], load_sem.at[3]),
        pltpu.make_async_copy(out_hbm, out_w, load_sem.at[4]),
        pltpu.make_async_copy(lateral_hbm, lat_w, load_sem.at[5]),
        pltpu.make_async_copy(conv_hbm, conv_w, load_sem.at[6]),
    ]
    for load in loads:
        load.start()

    fpad[...] = jnp.zeros_like(fpad)
    cpad[...] = jnp.zeros_like(cpad)

    barrier = pltpu.get_barrier_semaphore()

    def greet(to_blk, to_head):
        pl.semaphore_signal(barrier, inc=1, device_id={"blk": to_blk, "head": to_head})

    greet(blk, sib)
    greet(target, head)
    greet(source, head)

    has_up = blk > 0
    has_down = blk < count - 1

    @pl.when(has_up)
    def _():
        greet(blk - 1, head)
        greet(blk - 1, sib)

    @pl.when(has_down)
    def _():
        greet(blk + 1, head)
        greet(blk + 1, sib)

    pl.semaphore_wait(barrier, 3 + 2 * has_up.astype(jnp.int32) + 2 * has_down.astype(jnp.int32))

    def remote(src, dst, send, recv, to_blk, to_head):
        return pltpu.make_async_remote_copy(
            src_ref=src, dst_ref=dst, send_sem=send, recv_sem=recv,
            device_id={"blk": to_blk, "head": to_head},
        )

    tok_copy = remote(tokens_ref, tok.at[head], tok_sem.at[0], tok_sem.at[1], blk, sib)
    tok_copy.start()

    acc[...] = jnp.zeros_like(acc)
    total[...] = jnp.zeros_like(total)
    peak[...] = jnp.full(peak.shape, -jnp.inf, F32)

    def ring_copy(step, sub):
        return remote(
            ring.at[step, sub], ring.at[step + 1, sub],
            ring_send.at[step, sub], ring_recv.at[step + 1, sub], target, head,
        )

    def sib_copy(step, sub):
        return remote(
            ring.at[step, sub], other.at[step, sub],
            sib_send.at[step, sub], sib_recv.at[step, sub], blk, sib,
        )

    loads[0].wait()
    tok_copy.wait()
    left, right = tok[0], tok[1]
    width = left.shape[1] + right.shape[1]
    mean_row = (
        jnp.sum(left, axis=-1, keepdims=True) + jnp.sum(right, axis=-1, keepdims=True)
    ) / width
    left = left - mean_row
    right = right - mean_row
    spread = (
        jnp.sum(left * left, axis=-1, keepdims=True) + jnp.sum(right * right, axis=-1, keepdims=True)
    ) / width
    scale = lax.rsqrt(spread + 1e-06)
    gain = gain_ref[...]
    wide = left.shape[1]
    normed[:, :wide] = (left * scale * gain[:, :wide]).astype(BF16)
    normed[:, wide:] = (right * scale * gain[:, wide:]).astype(BF16)
    piece = half // SUBS
    for sub in range(SUBS):
        ring[0, sub] = normed[pl.ds(pl.multiple_of(head * half + sub * piece, 16), piece), :]
    for sub in range(SUBS):
        ring_copy(0, sub).start()
    for sub in range(SUBS):
        other[0, sub] = normed[pl.ds(pl.multiple_of(sib * half + sub * piece, 16), piece), :]

    loads[1].wait()
    wvt[...] = qkv[2].T
    loads[2].wait()
    queries = (dot(normed[...], qkv[0]) * (HEAD_DIM ** -0.5)).astype(BF16)
    per_pair = 2 * HEAD_DIM
    quad = qbd.shape[2]
    lane = lax.broadcasted_iota(jnp.int32, (rows, quad), 1)
    for pair in range(pairs):
        base = pair * per_pair // quad * quad
        block = queries[:, base : base + quad]
        for inner in range(2):
            first = pair * per_pair + inner * HEAD_DIM - base
            keep = (lane >= first) & (lane < first + HEAD_DIM)
            qbd[pair, inner * rows : (inner + 1) * rows, :] = jnp.where(keep, block, jnp.zeros_like(block))
    loads[3].wait()

    def project(step):
        chunk = jnp.concatenate(
            [ring[step].reshape(half, width), other[step].reshape(half, width)], axis=0
        )
        kbuf[...] = dot(chunk, qkv[1]).astype(BF16)
        vbuf[...] = dot_nt(wvt[...], chunk).astype(BF16)

    def attend():
        for pair in range(pairs):
            base = pair * per_pair // quad * quad
            scores = dot_nt(kbuf[:, base : base + quad], qbd[pair])
            before = peak[pair]
            now = jnp.maximum(before, jnp.max(scores, axis=0, keepdims=True))
            weights = jnp.exp(scores - now)
            factor = jnp.exp(before - now)
            peak[pair] = now
            total[pair] = total[pair] * factor + jnp.sum(weights, axis=0, keepdims=True)
            mixed = dot(vbuf[pair * per_pair : (pair + 1) * per_pair, :], weights.astype(BF16))
            acc[pair] = acc[pair] * factor + mixed

    def ring_step(step, carry):
        for sub in range(SUBS):
            ring_copy(step - 1, sub).wait_recv()

            @pl.when(step < count - 1)
            def _():
                ring_copy(step, sub).start()

            sib_copy(step, sub).start()
            if sub == 0:
                @pl.when(step > 1)
                def _():
                    for piece_sub in range(SUBS):
                        sib_copy(step - 1, piece_sub).wait_recv()

                project(step - 1)
            if sub == SUBS - 1:
                attend()
        return carry

    lax.fori_loop(1, count, ring_step, 0)
    for sub in range(SUBS):
        sib_copy(count - 1, sub).wait_recv()
    project(count - 1)
    attend()

    pair_lane = lax.broadcasted_iota(jnp.int32, (rows, per_pair), 1)
    for pair in range(pairs):
        done = (acc[pair] / total[pair]).T
        att[:, pair * per_pair : (pair + 1) * per_pair] = jnp.where(
            pair_lane < HEAD_DIM, done[:rows], done[rows:]
        ).astype(BF16)

    loads[4].wait()

    def tile_rows(ref, side):
        return jnp.concatenate(
            [
                ref[pl.ds(pl.multiple_of(side * cols + row * GW, 16), cols), :]
                for row in range(ROWS_DEV)
            ],
            axis=0,
        )

    part_send[...] = dot(tile_rows(att, sib), out_w[...]).astype(BF16)
    part_copy = remote(part_send, part_recv, part_sem.at[0], part_sem.at[1], blk, sib)
    part_copy.start()
    own = dot(tile_rows(att, head), out_w[...])
    residual = jnp.concatenate([tile_rows(tok.at[0], head), tile_rows(tok.at[1], head)], axis=1)
    own = own + residual
    loads[5].wait()
    loads[6].wait()
    part_copy.wait()
    block_out = (own + part_recv[...].astype(F32)).astype(BF16)

    cells = ROWS_DEV * cols
    gains = gains_ref[...]
    fine_in = layer_norm(dot(block_out, lat_w[0]), gains[0:1]).astype(BF16).astype(F32)
    for row in range(ROWS_DEV):
        fpad[1 + row, 8 : 8 + cols, :] = fine_in[row * cols : (row + 1) * cols]

    def halo(pad, first_row, last_row, inner, index):
        below = last_row + 1
        src_col = pl.multiple_of(inner - (inner - 8) * head, 8)
        dst_col = pl.multiple_of((8 + inner) * head, 8)
        tile = pl.ds(src_col, 8)
        into = pl.ds(dst_col, 8)
        body_cols = pl.ds(8, inner)

        def make(src, dst, place, to_blk, to_head):
            return remote(
                src, dst, halo_send.at[index + place], halo_recv.at[index + place], to_blk, to_head
            )

        span = pl.ds(first_row, last_row - first_row + 1)
        return [
            (None, make(pad.at[span, tile], pad.at[span, into], 0, blk, sib)),
            ("up", make(pad.at[first_row, body_cols], pad.at[below, body_cols], 1, blk - 1, head)),
            ("up", make(pad.at[first_row, tile], pad.at[below, into], 2, blk - 1, sib)),
            ("down", make(pad.at[last_row, body_cols], pad.at[0, body_cols], 3, blk + 1, head)),
            ("down", make(pad.at[last_row, tile], pad.at[0, into], 4, blk + 1, sib)),
        ]

    def guarded(way, action):
        if way is None:
            action()
        else:
            pl.when(has_up if way == "up" else has_down)(action)

    opposite = {None: None, "up": "down", "down": "up"}
    fine_halo = halo(fpad, 1, ROWS_DEV, cols, 0)
    for way, copy in fine_halo:
        guarded(way, copy.start)

    tall = block_out[:cols]
    for row in range(1, ROWS_DEV):
        tall = jnp.maximum(tall, block_out[row * cols : (row + 1) * cols])
    pool_rows = ccol.shape[0]
    at_row = lax.broadcasted_iota(jnp.int32, (pool_rows, cols), 0)
    at_col = lax.broadcasted_iota(jnp.int32, (pool_rows, cols), 1)
    pooled = jnp.maximum(
        dot((at_col == 2 * at_row).astype(F32).astype(BF16), tall),
        dot((at_col == 2 * at_row + 1).astype(F32).astype(BF16), tall),
    ).astype(BF16)
    coarse_cols = cols // 2
    coarse_in = layer_norm(dot(pooled, lat_w[1]), gains[2:3]).astype(BF16).astype(F32)
    cpad[1, 8 : 8 + coarse_cols, :] = coarse_in[:coarse_cols]
    coarse_halo = halo(cpad, 1, 1, coarse_cols, 5)
    for way, copy in coarse_halo:
        guarded(way, copy.start)

    channels = fine_ref.shape[-1]
    for way, copy in fine_halo:
        guarded(opposite[way], copy.wait_recv)
    for a in range(3):
        for b in range(3):
            place = (3 * a + b) * channels
            for row in range(ROWS_DEV):
                fcol[row * cols : (row + 1) * cols, place : place + channels] = fpad[
                    row + a, 7 + b : 7 + b + cols, :
                ].astype(BF16)
    fine_out = layer_norm(dot(fcol[...], conv_w[0]), gains[1:2]).astype(BF16)
    for row in range(ROWS_DEV):
        fine_ref[row] = fine_out[row * cols : (row + 1) * cols]

    for way, copy in coarse_halo:
        guarded(opposite[way], copy.wait_recv)
    for a in range(3):
        for b in range(3):
            place = (3 * a + b) * channels
            ccol[:, place : place + channels] = cpad[a, 7 + b : 7 + b + pool_rows, :].astype(BF16)
    coarse_out = layer_norm(dot(ccol[...], conv_w[1]), gains[3:4]).astype(BF16)
    coarse_ref[0] = coarse_out[:coarse_cols]

    for way, copy in fine_halo + coarse_halo:
        guarded(way, copy.wait_send)
    for sub in range(SUBS):
        ring_copy(0, sub).wait_send()

    def drain(step, carry):
        for sub in range(SUBS):
            sib_copy(step, sub).wait_send()

            @pl.when(step < count - 1)
            def _():
                ring_copy(step, sub).wait_send()

        return carry

    lax.fori_loop(1, count, drain, 0)


def body(tokens, norm_gain, qkv_weight, out_weight, lateral_weight, conv_weight, level_gains):
    count = lax.axis_size("blk")
    rows, wide = tokens.shape
    width = qkv_weight.shape[1]
    heads_width = qkv_weight.shape[2]
    channels = lateral_weight.shape[2]
    per_pair = 2 * HEAD_DIM
    pairs = heads_width // per_pair
    quad = 2 * per_pair
    half = rows // 2
    cols = GW // 2
    cells = ROWS_DEV * cols
    coarse_cols = cols // 2
    pool_rows = -(-coarse_cols // 16) * 16
    conv_depth = 9 * channels
    vmem = pl.BlockSpec(memory_space=pltpu.VMEM)
    hbm = pl.BlockSpec(memory_space=pl.ANY)
    dma = pltpu.SemaphoreType.DMA
    return pl.pallas_call(
        functools.partial(kernel, count),
        out_shape=(
            jax.ShapeDtypeStruct((ROWS_DEV, cols, channels), BF16),
            jax.ShapeDtypeStruct((ROWS_DEV // 2, coarse_cols, channels), BF16),
        ),
        in_specs=[hbm, vmem, hbm, hbm, hbm, hbm, vmem],
        out_specs=(vmem, vmem),
        scratch_shapes=[
            pltpu.VMEM((2, rows, wide), F32),
            pltpu.VMEM(qkv_weight.shape, BF16),
            pltpu.VMEM(out_weight.shape, BF16),
            pltpu.VMEM(lateral_weight.shape, BF16),
            pltpu.VMEM((2, conv_depth, channels), BF16),
            pltpu.VMEM((heads_width, width), BF16),
            pltpu.VMEM((rows, width), BF16),
            pltpu.VMEM((count, SUBS, half // SUBS, width), BF16),
            pltpu.VMEM((count, SUBS, half // SUBS, width), BF16),
            pltpu.VMEM((pairs, 2 * rows, quad), BF16),
            pltpu.VMEM((rows, heads_width), BF16),
            pltpu.VMEM((heads_width, rows), BF16),
            pltpu.VMEM((pairs, per_pair, 2 * rows), F32),
            pltpu.VMEM((pairs, 1, 2 * rows), F32),
            pltpu.VMEM((pairs, 1, 2 * rows), F32),
            pltpu.VMEM((rows, heads_width), BF16),
            pltpu.VMEM((cells, width), BF16),
            pltpu.VMEM((cells, width), BF16),
            pltpu.VMEM((ROWS_DEV + 2, cols + 16, channels), F32),
            pltpu.VMEM((3, pool_rows + 16, channels), F32),
            pltpu.VMEM((cells, conv_depth), BF16),
            pltpu.VMEM((pool_rows, conv_depth), BF16),
            dma((7,)),
            dma((2,)),
            dma((count, SUBS)),
            dma((count, SUBS)),
            dma((count, SUBS)),
            dma((count, SUBS)),
            dma((2,)),
            dma((10,)),
            dma((10,)),
        ],
        compiler_params=pltpu.CompilerParams(
            collective_id=0, has_side_effects=True, vmem_limit_bytes=50 * 1024 * 1024
        ),
    )(
        tokens,
        norm_gain.reshape(1, width),
        qkv_weight,
        out_weight,
        lateral_weight,
        conv_weight.reshape(2, conv_depth, channels),
        level_gains.reshape(4, channels),
    )


def solution(mesh):
    in_specs = (
        P(("groups", "blk"), "head"),
        P(),
        P(None, None, "head"),
        P("head", None),
        P(),
        P(),
        P(),
    )
    out_specs = (P(("groups", "blk"), "head", None), P(("groups", "blk"), "head", None))
    return jax.shard_map(body, mesh=mesh, in_specs=in_specs, out_specs=out_specs, check_vma=False)
```

time: 113 us -> 50.7 us (0.45)
  Pallas kernels: 0 us -> 43.2 us
  starting transfers between devices: 32.1 us -> 0 us
  waiting for transfers between devices: 16.8 us -> 0 us
  matrix products: 14.7 us -> 0 us
  blocking collectives: 14.4 us -> 0 us
  between operations: 14.5 us -> 0.64 us
  other arithmetic: 11.5 us -> 0 us
  local copies, waits for them, and re-layouts: 8.16 us -> 6.05 us
    pallas_call x0 -> x1, Pallas kernels: none -> 43.2 us  [body(): pl.pallas_call(functools.partial(kernel, count), out_shape=(jax.ShapeDtyp...]
    ppermute x8 -> x0, starting transfers between devices: 21.2 us -> none  [the longest x4 13.3 us: padded_2(): lax.ppermute(head, axis, [((i + 1) % count, i) for i in range(ends)])]
    dot_general x26 -> x0, matrix products: 14.7 us -> none  [the longest x18 2.98 us: conv_taps(): jnp.einsum('rcd,de->rce', window, kernel[tap_row, tap_col], preferred_ele...]
    all_to_all x1 -> x0, blocking collectives: 11.4 us -> none  [body(): lax.all_to_all(one_head.reshape(blk_count, slice_rows * HEAD_DIM), 'blk',...]
    all_to_all x2 -> x0, starting transfers between devices: 11 us -> none  [the longest x1 5.69 us: body(): lax.all_to_all(query_send, 'blk', split_axis=0, concat_axis=0, tiled=True)]
    reduce_scatter x1 -> x0, waiting for transfers between devices: 7.51 us -> none  [body(): lax.psum_scatter(partial_value.astype(jnp.bfloat16), 'head', scatter_dime...]
    all_to_all x2 -> x0, waiting for transfers between devices: 7.34 us -> none  [the longest x1 6.29 us: body(): lax.all_to_all(pair_send, 'blk', split_axis=0, concat_axis=0, tiled=True)]
    all_to_all x3 -> x0, other arithmetic: 4.12 us -> none  [the longest x2 2.96 us: body(): lax.all_to_all(query_send, 'blk', split_axis=0, concat_axis=0, tiled=True)]
  transfers between devices with their start and end apart: 11 -> 0, of which waited for: 5 -> 0; matrix products, arithmetic and copies ran while one was open for 12% -> 0% of each run, Pallas kernels for 0% -> 0%
where the time goes in v1:
time: 50.7 us; the launch traced here: 49.9 us
  Pallas kernels  43.2 us (85%)
  local copies, waits for them, and re-layouts  6.05 us (12%)
  between operations  0.64 us (1%)
    pallas_call x1, Pallas kernels, body(): pl.pallas_call(functools.partial(kernel, count), out_shape=(jax.ShapeDtyp...  43.2 us
    unnamed x10, local copies, waits for them, and re-layouts  5.35 us

profile of v1, /device:TPU:9, one launch (start us, length us, event | category | flops | bytes accessed | tf_op | source)
XLA Modules:
  0.0 49.9 jit_solution(13489509385985169782)
XLA Ops:
  0.6 0.7 %reshape.15.gains_ref = f32[4,256]{1,0:T(4,128)S(1)} reshape(f32[2,2,256]{2,1,0:T(2,128)} %param.13) | data formatting | bytes 8192 | tf_op jit(solution)/shard_map/reshape | solution.py:407
  1.3 0.0 copy-start
  1.3 1.2 %copy-done = bf16[512,1024]{1,0:T(8,128)(2,1)S(1)} copy-done((bf16[512,1024]{1,0:T(8,128)(2,1)S(1)}, bf16[512,1024]{1,0:T(8,128)(2,1)}, u32[]{:S(2)}) %copy-start) | copy-done | bytes 1048600
  2.6 0.0 copy-start.1
  2.6 1.2 %copy-done.1 = bf16[2,1024,256]{2,1,0:T(8,128)(2,1)S(1)} copy-done((bf16[2,1024,256]{2,1,0:T(8,128)(2,1)S(1)}, bf16[2,1024,256]{2,1,0:T(8,128)(2,1)}, u32[]{:S(2)}) %copy-start.1) | copy-done | bytes 1048600
  3.8 0.0 copy-start.2
  3.8 1.0 %copy-done.2 = f32[192,512]{1,0:T(8,128)S(1)} copy-done((f32[192,512]{1,0:T(8,128)S(1)}, f32[192,512]{1,0:T(8,128)}, u32[]{:S(2)}) %copy-start.2) | copy-done | bytes 393240
  4.8 0.0 copy-start.3
  4.8 0.7 %copy-done.3 = f32[1024]{0:T(1024)S(1)} copy-done((f32[1024]{0:T(1024)S(1)}, f32[1024]{0:T(1024)}, u32[]{:S(2)}) %copy-start.3) | copy-done | bytes 4120
  5.5 43.2 %shard_map.86 = (bf16[2,48,256]{2,1,0:T(8,128)(2,1)S(1)}, bf16[1,24,256]{2,1,0:T(8,128)(2,1)S(1)}) custom-call(f32[192,512]{1,0:T(8,128)S(1)} %copy-done.2, f32[1,1024]{1,0:T(1,128)S(1)} %bitcast.2, bf16[3,1024,512]{2,1,0:T(8,128)(2,1)} %qkv_hbm.1, bf16[512,1024]{1,0:T(8,128)(2,1)S(1)} %copy-done, bf16[2,1024,256]{2,1,0:T(8,128)(2,1)S(1)} %copy-done.1, ...), custom_call_target="tpu_custom_call" | custom-call | tf_op jit(solution)/shard_map/pallas_call | solution.py:356
  48.7 0.6 %copy.11 = bf16[2,48,256]{2,1,0:T(8,128)(2,1)} copy(bf16[2,48,256]{2,1,0:T(8,128)(2,1)S(1)} %get-tuple-element.4) | data formatting | bytes 98304
  49.3 0.6 %copy.12 = bf16[1,24,256]{2,1,0:T(8,128)(2,1)} copy(bf16[1,24,256]{2,1,0:T(8,128)(2,1)S(1)} %get-tuple-element.5) | data formatting | bytes 24576
Async XLA Ops:
  1.3 1.2 %copy-start = (bf16[512,1024]{1,0:T(8,128)(2,1)S(1)}, bf16[512,1024]{1,0:T(8,128)(2,1)}, u32[]{:S(2)}) copy-start(bf16[512,1024]{1,0:T(8,128)(2,1)} %out_hbm.1) | copy-start | bytes 3145732
  2.6 1.2 %copy-start.1 = (bf16[2,1024,256]{2,1,0:T(8,128)(2,1)S(1)}, bf16[2,1024,256]{2,1,0:T(8,128)(2,1)}, u32[]{:S(2)}) copy-start(bf16[2,1024,256]{2,1,0:T(8,128)(2,1)} %lateral_hbm.1) | copy-start | bytes 3145732
  3.8 1.0 %copy-start.2 = (f32[192,512]{1,0:T(8,128)S(1)}, f32[192,512]{1,0:T(8,128)}, u32[]{:S(2)}) copy-start(f32[192,512]{1,0:T(8,128)} %tokens_ref.1) | copy-start | bytes 1179652
  4.8 0.7 %copy-start.3 = (f32[1024]{0:T(1024)S(1)}, f32[1024]{0:T(1024)}, u32[]{:S(2)}) copy-start(f32[1024]{0:T(1024)} %param.8) | copy-start | bytes 12292

commit v2 on v1

--- a/solution.py
+++ b/solution.py
@@ -10,7 +10,7 @@
 HEAD_DIM = 64
 ROWS_DEV = 2
 GW = 96
-SUBS = 2
+SUBS = 4
 F32 = jnp.float32
 BF16 = jnp.bfloat16
 NT = (((1,), (1,)), ((), ()))
@@ -109,6 +109,8 @@
     acc[...] = jnp.zeros_like(acc)
     total[...] = jnp.zeros_like(total)
     peak[...] = jnp.full(peak.shape, -jnp.inf, F32)
+
+    last = count // 2
 
     def ring_copy(step, sub):
         return remote(
@@ -139,13 +141,12 @@
     wide = left.shape[1]
     normed[:, :wide] = (left * scale * gain[:, :wide]).astype(BF16)
     normed[:, wide:] = (right * scale * gain[:, wide:]).astype(BF16)
-    piece = half // SUBS
+    piece = rows // SUBS
     for sub in range(SUBS):
-        ring[0, sub] = normed[pl.ds(pl.multiple_of(head * half + sub * piece, 16), piece), :]
+        start = lax.rem(head * half + sub * piece, rows)
+        ring[0, sub] = normed[pl.ds(pl.multiple_of(start, 16), piece), :]
     for sub in range(SUBS):
         ring_copy(0, sub).start()
-    for sub in range(SUBS):
-        other[0, sub] = normed[pl.ds(pl.multiple_of(sib * half + sub * piece, 16), piece), :]
 
     loads[1].wait()
     wvt[...] = qkv[2].T
@@ -163,51 +164,93 @@
             qbd[pair, inner * rows : (inner + 1) * rows, :] = jnp.where(keep, block, jnp.zeros_like(block))
     loads[3].wait()
 
-    def project(step):
-        chunk = jnp.concatenate(
-            [ring[step].reshape(half, width), other[step].reshape(half, width)], axis=0
-        )
-        kbuf[...] = dot(chunk, qkv[1]).astype(BF16)
-        vbuf[...] = dot_nt(wvt[...], chunk).astype(BF16)
-
-    def attend():
-        for pair in range(pairs):
+    def keys_of(chunk):
+        kbuf[: chunk.shape[0], :] = dot(chunk, qkv[1]).astype(BF16)
+
+    def values_of(chunk):
+        vbuf[:, : chunk.shape[0]] = dot_nt(wvt[...], chunk).astype(BF16)
+
+    def attend(which, keys):
+        scores = []
+        for pair in which:
             base = pair * per_pair // quad * quad
-            scores = dot_nt(kbuf[:, base : base + quad], qbd[pair])
+            scores.append(dot_nt(kbuf[:keys, base : base + quad], qbd[pair]))
+        for pair, score in zip(which, scores):
             before = peak[pair]
-            now = jnp.maximum(before, jnp.max(scores, axis=0, keepdims=True))
-            weights = jnp.exp(scores - now)
+            now = jnp.maximum(before, jnp.max(score, axis=0, keepdims=True))
+            weights = jnp.exp(score - now)
             factor = jnp.exp(before - now)
             peak[pair] = now
             total[pair] = total[pair] * factor + jnp.sum(weights, axis=0, keepdims=True)
-            mixed = dot(vbuf[pair * per_pair : (pair + 1) * per_pair, :], weights.astype(BF16))
+            mixed = dot(
+                vbuf[pair * per_pair : (pair + 1) * per_pair, :keys], weights.astype(BF16)
+            )
             acc[pair] = acc[pair] * factor + mixed
 
-    def ring_step(step, carry):
-        for sub in range(SUBS):
-            ring_copy(step - 1, sub).wait_recv()
-
-            @pl.when(step < count - 1)
+    def own_chunk():
+        return ring[0].reshape(rows, width)
+
+    def two_chunks(step):
+        return jnp.concatenate(
+            [ring[step].reshape(rows, width), other[step].reshape(rows, width)], axis=0
+        )
+
+    def last_chunk():
+        return jnp.concatenate(
+            [
+                ring[last, : SUBS // 2].reshape(half, width),
+                other[last, : SUBS // 2].reshape(half, width),
+            ],
+            axis=0,
+        )
+
+    def arrive(step, sub):
+        ring_copy(step - 1, sub).wait_recv()
+        if sub < SUBS // 2:
+            @pl.when(step < last)
             def _():
                 ring_copy(step, sub).start()
-
-            sib_copy(step, sub).start()
-            if sub == 0:
-                @pl.when(step > 1)
-                def _():
-                    for piece_sub in range(SUBS):
-                        sib_copy(step - 1, piece_sub).wait_recv()
-
-                project(step - 1)
-            if sub == SUBS - 1:
-                attend()
+        else:
+            @pl.when(step < last - 1)
+            def _():
+                ring_copy(step, sub).start()
+        sib_copy(step, sub).start()
+
+    def met(step, subs):
+        for sub in range(subs):
+            sib_copy(step, sub).wait_recv()
+
+    low, high = range(pairs // 2), range(pairs // 2, pairs)
+
+    def hop(step, chunk_of, keys):
+        arrive(step, 0)
+        keys_of(chunk_of())
+        arrive(step, 1)
+        values_of(chunk_of())
+        arrive(step, 2)
+        attend(low, keys)
+        arrive(step, 3)
+        attend(high, keys)
+
+    hop(1, own_chunk, rows)
+
+    def ring_step(step, carry):
+        met(step - 1, SUBS)
+        hop(step, lambda: two_chunks(step - 1), 2 * rows)
         return carry
 
-    lax.fori_loop(1, count, ring_step, 0)
-    for sub in range(SUBS):
-        sib_copy(count - 1, sub).wait_recv()
-    project(count - 1)
-    attend()
+    lax.fori_loop(2, last, ring_step, 0)
+    met(last - 1, SUBS)
+    arrive(last, 0)
+    keys_of(two_chunks(last - 1))
+    arrive(last, 1)
+    values_of(two_chunks(last - 1))
+    attend(low, 2 * rows)
+    attend(high, 2 * rows)
+    met(last, SUBS // 2)
+    keys_of(last_chunk())
+    values_of(last_chunk())
+    attend(range(pairs), rows)
 
     pair_lane = lax.broadcasted_iota(jnp.int32, (rows, per_pair), 1)
     for pair in range(pairs):
@@ -239,8 +282,7 @@
     block_out = (own + part_recv[...].astype(F32)).astype(BF16)
 
     cells = ROWS_DEV * cols
-    gains = gains_ref[...]
-    fine_in = layer_norm(dot(block_out, lat_w[0]), gains[0:1]).astype(BF16).astype(F32)
+    fine_in = layer_norm(dot(block_out, lat_w[0]), gains_ref[0, 0:1]).astype(BF16).astype(F32)
     for row in range(ROWS_DEV):
         fpad[1 + row, 8 : 8 + cols, :] = fine_in[row * cols : (row + 1) * cols]
 
@@ -288,7 +330,7 @@
         dot((at_col == 2 * at_row + 1).astype(F32).astype(BF16), tall),
     ).astype(BF16)
     coarse_cols = cols // 2
-    coarse_in = layer_norm(dot(pooled, lat_w[1]), gains[2:3]).astype(BF16).astype(F32)
+    coarse_in = layer_norm(dot(pooled, lat_w[1]), gains_ref[1, 0:1]).astype(BF16).astype(F32)
     cpad[1, 8 : 8 + coarse_cols, :] = coarse_in[:coarse_cols]
     coarse_halo = halo(cpad, 1, 1, coarse_cols, 5)
     for way, copy in coarse_halo:
@@ -304,7 +346,7 @@
                 fcol[row * cols : (row + 1) * cols, place : place + channels] = fpad[
                     row + a, 7 + b : 7 + b + cols, :
                 ].astype(BF16)
-    fine_out = layer_norm(dot(fcol[...], conv_w[0]), gains[1:2]).astype(BF16)
+    fine_out = layer_norm(dot(fcol[...], conv_w[0]), gains_ref[0, 1:2]).astype(BF16)
     for row in range(ROWS_DEV):
         fine_ref[row] = fine_out[row * cols : (row + 1) * cols]
 
@@ -314,7 +356,7 @@
         for b in range(3):
             place = (3 * a + b) * channels
             ccol[:, place : place + channels] = cpad[a, 7 + b : 7 + b + pool_rows, :].astype(BF16)
-    coarse_out = layer_norm(dot(ccol[...], conv_w[1]), gains[3:4]).astype(BF16)
+    coarse_out = layer_norm(dot(ccol[...], conv_w[1]), gains_ref[1, 1:2]).astype(BF16)
     coarse_ref[0] = coarse_out[:coarse_cols]
 
     for way, copy in fine_halo + coarse_halo:
@@ -325,14 +367,18 @@
     def drain(step, carry):
         for sub in range(SUBS):
             sib_copy(step, sub).wait_send()
-
-            @pl.when(step < count - 1)
-            def _():
+            if sub < SUBS // 2:
                 ring_copy(step, sub).wait_send()
+            else:
+                @pl.when(step < last - 1)
+                def _():
+                    ring_copy(step, sub).wait_send()
 
         return carry
 
-    lax.fori_loop(1, count, drain, 0)
+    lax.fori_loop(1, last, drain, 0)
+    for sub in range(SUBS // 2):
+        sib_copy(last, sub).wait_send()
 
 
 def body(tokens, norm_gain, qkv_weight, out_weight, lateral_weight, conv_weight, level_gains):
@@ -344,7 +390,7 @@
     per_pair = 2 * HEAD_DIM
     pairs = heads_width // per_pair
     quad = 2 * per_pair
-    half = rows // 2
+    hops = count // 2 + 1
     cols = GW // 2
     cells = ROWS_DEV * cols
     coarse_cols = cols // 2
@@ -369,11 +415,11 @@
             pltpu.VMEM((2, conv_depth, channels), BF16),
             pltpu.VMEM((heads_width, width), BF16),
             pltpu.VMEM((rows, width), BF16),
-            pltpu.VMEM((count, SUBS, half // SUBS, width), BF16),
-            pltpu.VMEM((count, SUBS, half // SUBS, width), BF16),
+            pltpu.VMEM((hops, SUBS, rows // SUBS, width), BF16),
+            pltpu.VMEM((hops, SUBS, rows // SUBS, width), BF16),
             pltpu.VMEM((pairs, 2 * rows, quad), BF16),
-            pltpu.VMEM((rows, heads_width), BF16),
-            pltpu.VMEM((heads_width, rows), BF16),
+            pltpu.VMEM((2 * rows, heads_width), BF16),
+            pltpu.VMEM((heads_width, 2 * rows), BF16),
             pltpu.VMEM((pairs, per_pair, 2 * rows), F32),
             pltpu.VMEM((pairs, 1, 2 * rows), F32),
             pltpu.VMEM((pairs, 1, 2 * rows), F32),
@@ -386,16 +432,16 @@
             pltpu.VMEM((pool_rows, conv_depth), BF16),
             dma((7,)),
             dma((2,)),
-            dma((count, SUBS)),
-            dma((count, SUBS)),
-            dma((count, SUBS)),
-            dma((count, SUBS)),
+            dma((hops, SUBS)),
+            dma((hops, SUBS)),
+            dma((hops, SUBS)),
+            dma((hops, SUBS)),
             dma((2,)),
             dma((10,)),
             dma((10,)),
         ],
         compiler_params=pltpu.CompilerParams(
-            collective_id=0, has_side_effects=True, vmem_limit_bytes=50 * 1024 * 1024
+            collective_id=0, has_side_effects=True, vmem_limit_bytes=62 * 1024 * 1024
         ),
     )(
         tokens,
@@ -404,7 +450,7 @@
         out_weight,
         lateral_weight,
         conv_weight.reshape(2, conv_depth, channels),
-        level_gains.reshape(4, channels),
+        level_gains,
     )
 
 

time: 50.7 us -> 39.8 us (0.79)
  Pallas kernels: 43.2 us -> 36.1 us
  local copies, waits for them, and re-layouts: 6.05 us -> 2.73 us
    pallas_call x1, Pallas kernels: 43.2 us -> 36.1 us  [body(): pl.pallas_call(functools.partial(kernel, count), out_shape=(jax.ShapeDtyp...]
    unnamed x10 -> x2, local copies, waits for them, and re-layouts: 5.35 us -> 2.73 us
    reshape x1 -> x0, local copies, waits for them, and re-layouts: 0.7 us -> none  [body(): level_gains.reshape(4, channels)]
where the time goes in v2:
time: 39.8 us; the launch traced here: 39.5 us
  Pallas kernels  36.1 us (91%)
  local copies, waits for them, and re-layouts  2.73 us (7%)
  between operations  0.64 us (2%)
    pallas_call x1, Pallas kernels, body(): pl.pallas_call(functools.partial(kernel, count), out_shape=(jax.ShapeDtyp...  36.1 us
    unnamed x2, local copies, waits for them, and re-layouts  2.73 us

profile of v2, /device:TPU:9, one launch (start us, length us, event | category | flops | bytes accessed | tf_op | source)
XLA Modules:
  0.0 39.5 jit_solution(5940765226768991556)
XLA Ops:
  0.6 36.1 %shard_map.86 = (bf16[2,48,256]{2,1,0:T(8,128)(2,1)}, bf16[1,24,256]{2,1,0:T(8,128)(2,1)}) custom-call(f32[192,512]{1,0:T(8,128)} %tokens_ref.1, f32[1,1024]{1,0:T(1,128)} %bitcast.3, bf16[3,1024,512]{2,1,0:T(8,128)(2,1)} %qkv_hbm.1, bf16[512,1024]{1,0:T(8,128)(2,1)} %out_hbm.1, bf16[2,1024,256]{2,1,0:T(8,128)(2,1)} %lateral_hbm.1, ...), custom_call_target="tpu_custom_call" | custom-call | tf_op jit(solution)/shard_map/pallas_call | solution.py:402
  36.8 1.4 %copy.11 = bf16[2,48,256]{2,1,0:T(8,128)(2,1)} copy(bf16[2,48,256]{2,1,0:T(8,128)(2,1)} %get-tuple-element.4) | data formatting | bytes 98304
  38.2 1.3 %copy.12 = bf16[1,24,256]{2,1,0:T(8,128)(2,1)} copy(bf16[1,24,256]{2,1,0:T(8,128)(2,1)} %get-tuple-element.5) | data formatting | bytes 24576

commit v3 on v2

--- a/solution.py
+++ b/solution.py
@@ -35,7 +35,7 @@
     count,
     tokens_ref, gain_ref, qkv_hbm, out_hbm, lateral_hbm, conv_hbm, gains_ref,
     fine_ref, coarse_ref,
-    tok, qkv, out_w, lat_w, conv_w, wvt, normed, ring, other, qbd, kbuf, vbuf,
+    tok, qkv, out_w, lat_w, conv_w, normed, ring, other, qbd, kbuf, vbuf,
     acc, peak, total, att, part_send, part_recv, fpad, cpad, fcol, ccol,
     load_sem, tok_sem, ring_send, ring_recv, sib_send, sib_recv, part_sem, halo_send, halo_recv,
 ):
@@ -60,9 +60,9 @@
 
     loads = [
         pltpu.make_async_copy(tokens_ref, tok.at[head], load_sem.at[0]),
-        pltpu.make_async_copy(qkv_hbm.at[2], qkv.at[2], load_sem.at[1]),
-        pltpu.make_async_copy(qkv_hbm.at[0], qkv.at[0], load_sem.at[2]),
-        pltpu.make_async_copy(qkv_hbm.at[1], qkv.at[1], load_sem.at[3]),
+        pltpu.make_async_copy(qkv_hbm.at[0], qkv.at[0], load_sem.at[1]),
+        pltpu.make_async_copy(qkv_hbm.at[1], qkv.at[1], load_sem.at[2]),
+        pltpu.make_async_copy(qkv_hbm.at[2], qkv.at[2], load_sem.at[3]),
         pltpu.make_async_copy(out_hbm, out_w, load_sem.at[4]),
         pltpu.make_async_copy(lateral_hbm, lat_w, load_sem.at[5]),
         pltpu.make_async_copy(conv_hbm, conv_w, load_sem.at[6]),
@@ -148,27 +148,11 @@
     for sub in range(SUBS):
         ring_copy(0, sub).start()
 
-    loads[1].wait()
-    wvt[...] = qkv[2].T
-    loads[2].wait()
-    queries = (dot(normed[...], qkv[0]) * (HEAD_DIM ** -0.5)).astype(BF16)
-    per_pair = 2 * HEAD_DIM
-    quad = qbd.shape[2]
-    lane = lax.broadcasted_iota(jnp.int32, (rows, quad), 1)
-    for pair in range(pairs):
-        base = pair * per_pair // quad * quad
-        block = queries[:, base : base + quad]
-        for inner in range(2):
-            first = pair * per_pair + inner * HEAD_DIM - base
-            keep = (lane >= first) & (lane < first + HEAD_DIM)
-            qbd[pair, inner * rows : (inner + 1) * rows, :] = jnp.where(keep, block, jnp.zeros_like(block))
-    loads[3].wait()
-
     def keys_of(chunk):
         kbuf[: chunk.shape[0], :] = dot(chunk, qkv[1]).astype(BF16)
 
     def values_of(chunk):
-        vbuf[:, : chunk.shape[0]] = dot_nt(wvt[...], chunk).astype(BF16)
+        vbuf[:, : chunk.shape[0]] = dot(chunk, qkv[2]).astype(BF16).T
 
     def attend(which, keys):
         scores = []
@@ -232,7 +216,28 @@
         arrive(step, 3)
         attend(high, keys)
 
-    hop(1, own_chunk, rows)
+    loads[1].wait()
+    queries = (dot(normed[...], qkv[0]) * (HEAD_DIM ** -0.5)).astype(BF16)
+    per_pair = 2 * HEAD_DIM
+    quad = qbd.shape[2]
+    lane = lax.broadcasted_iota(jnp.int32, (rows, quad), 1)
+    for pair in range(pairs):
+        base = pair * per_pair // quad * quad
+        block = queries[:, base : base + quad]
+        for inner in range(2):
+            first = pair * per_pair + inner * HEAD_DIM - base
+            keep = (lane >= first) & (lane < first + HEAD_DIM)
+            qbd[pair, inner * rows : (inner + 1) * rows, :] = jnp.where(keep, block, jnp.zeros_like(block))
+    arrive(1, 0)
+    loads[2].wait()
+    keys_of(own_chunk())
+    arrive(1, 1)
+    loads[3].wait()
+    values_of(own_chunk())
+    arrive(1, 2)
+    attend(low, rows)
+    arrive(1, 3)
+    attend(high, rows)
 
     def ring_step(step, carry):
         met(step - 1, SUBS)
@@ -379,6 +384,17 @@
     lax.fori_loop(1, last, drain, 0)
     for sub in range(SUBS // 2):
         sib_copy(last, sub).wait_send()
+
+
+def deliver(fine_in, coarse_in, fine_out, coarse_out, sem):
+    copies = [
+        pltpu.make_async_copy(fine_in, fine_out, sem.at[0]),
+        pltpu.make_async_copy(coarse_in, coarse_out, sem.at[1]),
+    ]
+    for copy in copies:
+        copy.start()
+    for copy in copies:
+        copy.wait()
 
 
 def body(tokens, norm_gain, qkv_weight, out_weight, lateral_weight, conv_weight, level_gains):
@@ -399,7 +415,7 @@
     vmem = pl.BlockSpec(memory_space=pltpu.VMEM)
     hbm = pl.BlockSpec(memory_space=pl.ANY)
     dma = pltpu.SemaphoreType.DMA
-    return pl.pallas_call(
+    maps = pl.pallas_call(
         functools.partial(kernel, count),
         out_shape=(
             jax.ShapeDtypeStruct((ROWS_DEV, cols, channels), BF16),
@@ -413,7 +429,6 @@
             pltpu.VMEM(out_weight.shape, BF16),
             pltpu.VMEM(lateral_weight.shape, BF16),
             pltpu.VMEM((2, conv_depth, channels), BF16),
-            pltpu.VMEM((heads_width, width), BF16),
             pltpu.VMEM((rows, width), BF16),
             pltpu.VMEM((hops, SUBS, rows // SUBS, width), BF16),
             pltpu.VMEM((hops, SUBS, rows // SUBS, width), BF16),
@@ -452,6 +467,13 @@
         conv_weight.reshape(2, conv_depth, channels),
         level_gains,
     )
+    return pl.pallas_call(
+        deliver,
+        out_shape=tuple(jax.ShapeDtypeStruct(each.shape, each.dtype) for each in maps),
+        in_specs=[hbm, hbm],
+        out_specs=(hbm, hbm),
+        scratch_shapes=[dma((2,))],
+    )(*maps)
 
 
 def solution(mesh):

time: 39.8 us -> 39.9 us (level)
  Pallas kernels: 36.1 us -> 39 us
  local copies, waits for them, and re-layouts: 2.73 us -> 0 us
    pallas_call x0 -> x1, Pallas kernels: none -> 2.98 us  [body(): pl.pallas_call(deliver, out_shape=tuple((jax.ShapeDtypeStruct(each.shape,...]
    unnamed x2 -> x0, local copies, waits for them, and re-layouts: 2.73 us -> none
where the time goes in v3:
time: 39.9 us; the launch traced here: 39.6 us
  Pallas kernels  39 us (98%)
  between operations  0.64 us (2%)
    pallas_call x1, Pallas kernels, body(): pl.pallas_call(functools.partial(kernel, count), out_shape=(jax.ShapeDtyp...  36 us
    pallas_call x1, Pallas kernels, body(): pl.pallas_call(deliver, out_shape=tuple((jax.ShapeDtypeStruct(each.shape,...  2.98 us

profile of v3, /device:TPU:9, one launch (start us, length us, event | category | flops | bytes accessed | tf_op | source)
XLA Modules:
  0.0 39.6 jit_solution(2536112221839992643)
XLA Ops:
  0.6 36.0 %shard_map.86 = (bf16[2,48,256]{2,1,0:T(8,128)(2,1)}, bf16[1,24,256]{2,1,0:T(8,128)(2,1)}) custom-call(f32[192,512]{1,0:T(8,128)} %tokens_ref.1, f32[1,1024]{1,0:T(1,128)} %bitcast.3, bf16[3,1024,512]{2,1,0:T(8,128)(2,1)} %qkv_hbm.1, bf16[512,1024]{1,0:T(8,128)(2,1)} %out_hbm.1, bf16[2,1024,256]{2,1,0:T(8,128)(2,1)} %lateral_hbm.1, ...), custom_call_target="tpu_custom_call" | custom-call | tf_op jit(solution)/shard_map/pallas_call | solution.py:418
  36.7 3.0 %shard_map.87 = (bf16[2,48,256]{2,1,0:T(8,128)(2,1)}, bf16[1,24,256]{2,1,0:T(8,128)(2,1)}) custom-call(bf16[2,48,256]{2,1,0:T(8,128)(2,1)} %get-tuple-element.4.fine_in, bf16[1,24,256]{2,1,0:T(8,128)(2,1)} %get-tuple-element.5.coarse_in), custom_call_target="tpu_custom_call" | custom-call | tf_op jit(solution)/shard_map/pallas_call | solution.py:470

commit v4 on v3

--- a/solution.py
+++ b/solution.py
@@ -37,7 +37,7 @@
     fine_ref, coarse_ref,
     tok, qkv, out_w, lat_w, conv_w, normed, ring, other, qbd, kbuf, vbuf,
     acc, peak, total, att, part_send, part_recv, fpad, cpad, fcol, ccol,
-    load_sem, tok_sem, ring_send, ring_recv, sib_send, sib_recv, part_sem, halo_send, halo_recv,
+    load_sem, tok_send, tok_recv, ring_send, ring_recv, sib_send, sib_recv, part_sem, halo_send, halo_recv,
 ):
     blk = lax.axis_index("blk")
     head = lax.axis_index("head")
@@ -58,16 +58,28 @@
     target = jnp.where(head == 0, up_ring, down_ring)
     source = jnp.where(head == 0, down_ring, up_ring)
 
+    piece = rows // SUBS
+
+    def piece_rows(side, sub):
+        start = lax.rem(side * half + sub * piece, rows)
+        return pl.ds(pl.multiple_of(start, 16), piece)
+
     loads = [
-        pltpu.make_async_copy(tokens_ref, tok.at[head], load_sem.at[0]),
-        pltpu.make_async_copy(qkv_hbm.at[0], qkv.at[0], load_sem.at[1]),
-        pltpu.make_async_copy(qkv_hbm.at[1], qkv.at[1], load_sem.at[2]),
-        pltpu.make_async_copy(qkv_hbm.at[2], qkv.at[2], load_sem.at[3]),
-        pltpu.make_async_copy(out_hbm, out_w, load_sem.at[4]),
-        pltpu.make_async_copy(lateral_hbm, lat_w, load_sem.at[5]),
-        pltpu.make_async_copy(conv_hbm, conv_w, load_sem.at[6]),
+        pltpu.make_async_copy(
+            tokens_ref.at[piece_rows(head, sub)], tok.at[head, piece_rows(head, sub)],
+            load_sem.at[6 + sub],
+        )
+        for sub in range(SUBS)
     ]
-    for load in loads:
+    weights_in = [
+        pltpu.make_async_copy(qkv_hbm.at[0], qkv.at[0], load_sem.at[0]),
+        pltpu.make_async_copy(qkv_hbm.at[1], qkv.at[1], load_sem.at[1]),
+        pltpu.make_async_copy(qkv_hbm.at[2], qkv.at[2], load_sem.at[2]),
+        pltpu.make_async_copy(out_hbm, out_w, load_sem.at[3]),
+        pltpu.make_async_copy(lateral_hbm, lat_w, load_sem.at[4]),
+        pltpu.make_async_copy(conv_hbm, conv_w, load_sem.at[5]),
+    ]
+    for load in loads + weights_in:
         load.start()
 
     fpad[...] = jnp.zeros_like(fpad)
@@ -103,8 +115,22 @@
             device_id={"blk": to_blk, "head": to_head},
         )
 
-    tok_copy = remote(tokens_ref, tok.at[head], tok_sem.at[0], tok_sem.at[1], blk, sib)
-    tok_copy.start()
+    tok_out = [
+        remote(
+            tokens_ref.at[piece_rows(sib, sub)], tok.at[head, piece_rows(sib, sub)],
+            tok_send.at[sub], tok_recv.at[sub], blk, sib,
+        )
+        for sub in range(SUBS)
+    ]
+    for copy in tok_out:
+        copy.start()
+    tok_in = [
+        remote(
+            tokens_ref.at[piece_rows(head, sub)], tok.at[sib, piece_rows(head, sub)],
+            tok_send.at[sub], tok_recv.at[sub], blk, sib,
+        )
+        for sub in range(SUBS)
+    ]
 
     acc[...] = jnp.zeros_like(acc)
     total[...] = jnp.zeros_like(total)
@@ -124,29 +150,29 @@
             sib_send.at[step, sub], sib_recv.at[step, sub], blk, sib,
         )
 
-    loads[0].wait()
-    tok_copy.wait()
-    left, right = tok[0], tok[1]
-    width = left.shape[1] + right.shape[1]
-    mean_row = (
-        jnp.sum(left, axis=-1, keepdims=True) + jnp.sum(right, axis=-1, keepdims=True)
-    ) / width
-    left = left - mean_row
-    right = right - mean_row
-    spread = (
-        jnp.sum(left * left, axis=-1, keepdims=True) + jnp.sum(right * right, axis=-1, keepdims=True)
-    ) / width
-    scale = lax.rsqrt(spread + 1e-06)
     gain = gain_ref[...]
-    wide = left.shape[1]
-    normed[:, :wide] = (left * scale * gain[:, :wide]).astype(BF16)
-    normed[:, wide:] = (right * scale * gain[:, wide:]).astype(BF16)
-    piece = rows // SUBS
+    wide = tok.shape[2]
+    width = 2 * wide
     for sub in range(SUBS):
-        start = lax.rem(head * half + sub * piece, rows)
-        ring[0, sub] = normed[pl.ds(pl.multiple_of(start, 16), piece), :]
+        here = piece_rows(head, sub)
+        loads[sub].wait()
+        tok_in[sub].wait_recv()
+        left, right = tok[0, here, :], tok[1, here, :]
+        mean_row = (
+            jnp.sum(left, axis=-1, keepdims=True) + jnp.sum(right, axis=-1, keepdims=True)
+        ) / width
+        left = left - mean_row
+        right = right - mean_row
+        spread = (
+            jnp.sum(left * left, axis=-1, keepdims=True)
+            + jnp.sum(right * right, axis=-1, keepdims=True)
+        ) / width
+        scale = lax.rsqrt(spread + 1e-06)
+        ring[0, sub, :, :wide] = (left * scale * gain[:, :wide]).astype(BF16)
+        ring[0, sub, :, wide:] = (right * scale * gain[:, wide:]).astype(BF16)
+        ring_copy(0, sub).start()
     for sub in range(SUBS):
-        ring_copy(0, sub).start()
+        normed[piece_rows(head, sub), :] = ring[0, sub]
 
     def keys_of(chunk):
         kbuf[: chunk.shape[0], :] = dot(chunk, qkv[1]).astype(BF16)
@@ -179,13 +205,10 @@
             [ring[step].reshape(rows, width), other[step].reshape(rows, width)], axis=0
         )
 
-    def last_chunk():
+    def part_chunk(step, first):
+        subs = slice(first, first + SUBS // 2)
         return jnp.concatenate(
-            [
-                ring[last, : SUBS // 2].reshape(half, width),
-                other[last, : SUBS // 2].reshape(half, width),
-            ],
-            axis=0,
+            [ring[step, subs].reshape(half, width), other[step, subs].reshape(half, width)], axis=0
         )
 
     def arrive(step, sub):
@@ -200,8 +223,8 @@
                 ring_copy(step, sub).start()
         sib_copy(step, sub).start()
 
-    def met(step, subs):
-        for sub in range(subs):
+    def met(step, first, past):
+        for sub in range(first, past):
             sib_copy(step, sub).wait_recv()
 
     low, high = range(pairs // 2), range(pairs // 2, pairs)
@@ -216,7 +239,7 @@
         arrive(step, 3)
         attend(high, keys)
 
-    loads[1].wait()
+    weights_in[0].wait()
     queries = (dot(normed[...], qkv[0]) * (HEAD_DIM ** -0.5)).astype(BF16)
     per_pair = 2 * HEAD_DIM
     quad = qbd.shape[2]
@@ -229,10 +252,10 @@
             keep = (lane >= first) & (lane < first + HEAD_DIM)
             qbd[pair, inner * rows : (inner + 1) * rows, :] = jnp.where(keep, block, jnp.zeros_like(block))
     arrive(1, 0)
-    loads[2].wait()
+    weights_in[1].wait()
     keys_of(own_chunk())
     arrive(1, 1)
-    loads[3].wait()
+    weights_in[2].wait()
     values_of(own_chunk())
     arrive(1, 2)
     attend(low, rows)
@@ -240,21 +263,25 @@
     attend(high, rows)
 
     def ring_step(step, carry):
-        met(step - 1, SUBS)
+        met(step - 1, 0, SUBS)
         hop(step, lambda: two_chunks(step - 1), 2 * rows)
         return carry
 
     lax.fori_loop(2, last, ring_step, 0)
-    met(last - 1, SUBS)
+    mid = SUBS // 2
+    met(last - 1, 0, mid)
+    keys_of(part_chunk(last - 1, 0))
+    values_of(part_chunk(last - 1, 0))
+    attend(range(pairs), rows)
     arrive(last, 0)
-    keys_of(two_chunks(last - 1))
+    met(last - 1, mid, SUBS)
+    keys_of(part_chunk(last - 1, mid))
+    values_of(part_chunk(last - 1, mid))
     arrive(last, 1)
-    values_of(two_chunks(last - 1))
-    attend(low, 2 * rows)
-    attend(high, 2 * rows)
-    met(last, SUBS // 2)
-    keys_of(last_chunk())
-    values_of(last_chunk())
+    attend(range(pairs), rows)
+    met(last, 0, mid)
+    keys_of(part_chunk(last, 0))
+    values_of(part_chunk(last, 0))
     attend(range(pairs), rows)
 
     pair_lane = lax.broadcasted_iota(jnp.int32, (rows, per_pair), 1)
@@ -264,7 +291,7 @@
             pair_lane < HEAD_DIM, done[:rows], done[rows:]
         ).astype(BF16)
 
-    loads[4].wait()
+    weights_in[3].wait()
 
     def tile_rows(ref, side):
         return jnp.concatenate(
@@ -281,8 +308,8 @@
     own = dot(tile_rows(att, head), out_w[...])
     residual = jnp.concatenate([tile_rows(tok.at[0], head), tile_rows(tok.at[1], head)], axis=1)
     own = own + residual
-    loads[5].wait()
-    loads[6].wait()
+    weights_in[4].wait()
+    weights_in[5].wait()
     part_copy.wait()
     block_out = (own + part_recv[...].astype(F32)).astype(BF16)
 
@@ -367,6 +394,7 @@
     for way, copy in fine_halo + coarse_halo:
         guarded(way, copy.wait_send)
     for sub in range(SUBS):
+        tok_out[sub].wait_send()
         ring_copy(0, sub).wait_send()
 
     def drain(step, carry):
@@ -384,17 +412,6 @@
     lax.fori_loop(1, last, drain, 0)
     for sub in range(SUBS // 2):
         sib_copy(last, sub).wait_send()
-
-
-def deliver(fine_in, coarse_in, fine_out, coarse_out, sem):
-    copies = [
-        pltpu.make_async_copy(fine_in, fine_out, sem.at[0]),
-        pltpu.make_async_copy(coarse_in, coarse_out, sem.at[1]),
-    ]
-    for copy in copies:
-        copy.start()
-    for copy in copies:
-        copy.wait()
 
 
 def body(tokens, norm_gain, qkv_weight, out_weight, lateral_weight, conv_weight, level_gains):
@@ -415,7 +432,7 @@
     vmem = pl.BlockSpec(memory_space=pltpu.VMEM)
     hbm = pl.BlockSpec(memory_space=pl.ANY)
     dma = pltpu.SemaphoreType.DMA
-    maps = pl.pallas_call(
+    return pl.pallas_call(
         functools.partial(kernel, count),
         out_shape=(
             jax.ShapeDtypeStruct((ROWS_DEV, cols, channels), BF16),
@@ -445,8 +462,9 @@
             pltpu.VMEM((3, pool_rows + 16, channels), F32),
             pltpu.VMEM((cells, conv_depth), BF16),
             pltpu.VMEM((pool_rows, conv_depth), BF16),
-            dma((7,)),
-            dma((2,)),
+            dma((6 + SUBS,)),
+            dma((SUBS,)),
+            dma((SUBS,)),
             dma((hops, SUBS)),
             dma((hops, SUBS)),
             dma((hops, SUBS)),
@@ -456,7 +474,7 @@
             dma((10,)),
         ],
         compiler_params=pltpu.CompilerParams(
-            collective_id=0, has_side_effects=True, vmem_limit_bytes=62 * 1024 * 1024
+            collective_id=0, has_side_effects=True, vmem_limit_bytes=54912 * 1024
         ),
     )(
         tokens,
@@ -467,13 +485,6 @@
         conv_weight.reshape(2, conv_depth, channels),
         level_gains,
     )
-    return pl.pallas_call(
-        deliver,
-        out_shape=tuple(jax.ShapeDtypeStruct(each.shape, each.dtype) for each in maps),
-        in_specs=[hbm, hbm],
-        out_specs=(hbm, hbm),
-        scratch_shapes=[dma((2,))],
-    )(*maps)
 
 
 def solution(mesh):

time: 39.9 us -> 37.3 us (0.935)
  Pallas kernels: 39 us -> 33.8 us
  local copies, waits for them, and re-layouts: 0 us -> 2.59 us
    pallas_call x1 -> x0, Pallas kernels: 2.98 us -> none  [body(): pl.pallas_call(deliver, out_shape=tuple((jax.ShapeDtypeStruct(each.shape,...]
    unnamed x0 -> x6, local copies, waits for them, and re-layouts: none -> 2.59 us
    pallas_call x1, Pallas kernels: 36 us -> 33.8 us  [body(): pl.pallas_call(functools.partial(kernel, count), out_shape=(jax.ShapeDtyp...]
where the time goes in v4:
time: 37.3 us; the launch traced here: 37 us
  Pallas kernels  33.8 us (91%)
  local copies, waits for them, and re-layouts  2.59 us (7%)
  between operations  0.65 us (2%)
    pallas_call x1, Pallas kernels, body(): pl.pallas_call(functools.partial(kernel, count), out_shape=(jax.ShapeDtyp...  33.8 us
    unnamed x6, local copies, waits for them, and re-layouts  2.59 us

profile of v4, /device:TPU:9, one launch (start us, length us, event | category | flops | bytes accessed | tf_op | source)
XLA Modules:
  0.0 37.0 jit_solution(15223370584636216774)
XLA Ops:
  0.6 0.0 copy-start
  0.6 0.7 %copy-done = f32[1024]{0:T(1024)S(1)} copy-done((f32[1024]{0:T(1024)S(1)}, f32[1024]{0:T(1024)}, u32[]{:S(2)}) %copy-start) | copy-done | bytes 4120
  1.3 0.0 copy-start.1
  1.3 0.7 %copy-done.1 = f32[2,2,256]{2,1,0:T(2,128)S(1)} copy-done((f32[2,2,256]{2,1,0:T(2,128)S(1)}, f32[2,2,256]{2,1,0:T(2,128)}, u32[]{:S(2)}) %copy-start.1) | copy-done | bytes 4120
  2.0 33.8 %shard_map.86 = (bf16[2,48,256]{2,1,0:T(8,128)(2,1)S(1)}, bf16[1,24,256]{2,1,0:T(8,128)(2,1)S(1)}) custom-call(f32[192,512]{1,0:T(8,128)} %tokens_ref.1, f32[1,1024]{1,0:T(1,128)S(1)} %bitcast.2, bf16[3,1024,512]{2,1,0:T(8,128)(2,1)} %qkv_hbm.1, bf16[512,1024]{1,0:T(8,128)(2,1)} %out_hbm.1, bf16[2,1024,256]{2,1,0:T(8,128)(2,1)} %lateral_hbm.1, ...), custom_call_target="tpu_custom_call" | custom-call | tf_op jit(solution)/shard_map/pallas_call | solution.py:435
  35.8 0.6 %copy.11 = bf16[2,48,256]{2,1,0:T(8,128)(2,1)} copy(bf16[2,48,256]{2,1,0:T(8,128)(2,1)S(1)} %get-tuple-element.4) | data formatting | bytes 98304
  36.4 0.6 %copy.12 = bf16[1,24,256]{2,1,0:T(8,128)(2,1)} copy(bf16[1,24,256]{2,1,0:T(8,128)(2,1)S(1)} %get-tuple-element.5) | data formatting | bytes 24576
Async XLA Ops:
  0.6 0.7 %copy-start = (f32[1024]{0:T(1024)S(1)}, f32[1024]{0:T(1024)}, u32[]{:S(2)}) copy-start(f32[1024]{0:T(1024)} %param.8) | copy-start | bytes 12292
  1.3 0.7 %copy-start.1 = (f32[2,2,256]{2,1,0:T(2,128)S(1)}, f32[2,2,256]{2,1,0:T(2,128)}, u32[]{:S(2)}) copy-start(f32[2,2,256]{2,1,0:T(2,128)} %gains_ref.1) | copy-start | bytes 12292

commit v5 on v4

--- a/solution.py
+++ b/solution.py
@@ -33,9 +33,9 @@
 
 def kernel(
     count,
-    tokens_ref, gain_ref, qkv_hbm, out_hbm, lateral_hbm, conv_hbm, gains_ref,
+    tokens_ref, gain_hbm, qkv_hbm, out_hbm, lateral_hbm, conv_hbm, gains_hbm,
     fine_ref, coarse_ref,
-    tok, qkv, out_w, lat_w, conv_w, normed, ring, other, qbd, kbuf, vbuf,
+    gain_ref, gains_ref, tok, qkv, out_w, lat_w, conv_w, normed, ring, other, qbd, kbuf, vbuf,
     acc, peak, total, att, part_send, part_recv, fpad, cpad, fcol, ccol,
     load_sem, tok_send, tok_recv, ring_send, ring_recv, sib_send, sib_recv, part_sem, halo_send, halo_recv,
 ):
@@ -78,6 +78,8 @@
         pltpu.make_async_copy(out_hbm, out_w, load_sem.at[3]),
         pltpu.make_async_copy(lateral_hbm, lat_w, load_sem.at[4]),
         pltpu.make_async_copy(conv_hbm, conv_w, load_sem.at[5]),
+        pltpu.make_async_copy(gains_hbm, gains_ref, load_sem.at[6 + SUBS]),
+        pltpu.make_async_copy(gain_hbm, gain_ref, load_sem.at[7 + SUBS]),
     ]
     for load in loads + weights_in:
         load.start()
@@ -138,11 +140,33 @@
 
     last = count // 2
 
+    class Together:
+        def __init__(self, copies):
+            self.copies = copies
+
+        def start(self):
+            for copy in self.copies:
+                copy.start()
+
+        def wait_send(self):
+            for copy in self.copies:
+                copy.wait_send()
+
+        def wait_recv(self):
+            for copy in self.copies:
+                copy.wait_recv()
+
     def ring_copy(step, sub):
-        return remote(
-            ring.at[step, sub], ring.at[step + 1, sub],
-            ring_send.at[step, sub], ring_recv.at[step + 1, sub], target, head,
-        )
+        copies = []
+        for side in range(2):
+            span = pl.ds(side * tok.shape[2], tok.shape[2])
+            copies.append(
+                remote(
+                    ring.at[step, sub, :, span], ring.at[step + 1, sub, :, span],
+                    ring_send.at[step, sub, side], ring_recv.at[step + 1, sub, side], target, head,
+                )
+            )
+        return Together(copies)
 
     def sib_copy(step, sub):
         return remote(
@@ -150,6 +174,7 @@
             sib_send.at[step, sub], sib_recv.at[step, sub], blk, sib,
         )
 
+    weights_in[7].wait()
     gain = gain_ref[...]
     wide = tok.shape[2]
     width = 2 * wide
@@ -310,6 +335,7 @@
     own = own + residual
     weights_in[4].wait()
     weights_in[5].wait()
+    weights_in[6].wait()
     part_copy.wait()
     block_out = (own + part_recv[...].astype(F32)).astype(BF16)
 
@@ -438,9 +464,11 @@
             jax.ShapeDtypeStruct((ROWS_DEV, cols, channels), BF16),
             jax.ShapeDtypeStruct((ROWS_DEV // 2, coarse_cols, channels), BF16),
         ),
-        in_specs=[hbm, vmem, hbm, hbm, hbm, hbm, vmem],
+        in_specs=[hbm] * 7,
         out_specs=(vmem, vmem),
         scratch_shapes=[
+            pltpu.VMEM((1, width), F32),
+            pltpu.VMEM(level_gains.shape, F32),
             pltpu.VMEM((2, rows, wide), F32),
             pltpu.VMEM(qkv_weight.shape, BF16),
             pltpu.VMEM(out_weight.shape, BF16),
@@ -462,11 +490,11 @@
             pltpu.VMEM((3, pool_rows + 16, channels), F32),
             pltpu.VMEM((cells, conv_depth), BF16),
             pltpu.VMEM((pool_rows, conv_depth), BF16),
-            dma((6 + SUBS,)),
+            dma((8 + SUBS,)),
             dma((SUBS,)),
             dma((SUBS,)),
-            dma((hops, SUBS)),
-            dma((hops, SUBS)),
+            dma((hops, SUBS, 2)),
+            dma((hops, SUBS, 2)),
             dma((hops, SUBS)),
             dma((hops, SUBS)),
             dma((2,)),

time: 37.3 us -> 37.7 us (1.011)
  Pallas kernels: 33.8 us -> 34.2 us
    pallas_call x1, Pallas kernels: 33.8 us -> 34.2 us  [body(): pl.pallas_call(functools.partial(kernel, count), out_shape=(jax.ShapeDtyp...]
where the time goes in v5:
time: 37.7 us; the launch traced here: 37.4 us
  Pallas kernels  34.2 us (91%)
  local copies, waits for them, and re-layouts  2.59 us (7%)
  between operations  0.65 us (2%)
    pallas_call x1, Pallas kernels, body(): pl.pallas_call(functools.partial(kernel, count), out_shape=(jax.ShapeDtyp...  34.2 us
    unnamed x6, local copies, waits for them, and re-layouts  2.59 us

profile of v5, /device:TPU:9, one launch (start us, length us, event | category | flops | bytes accessed | tf_op | source)
XLA Modules:
  0.0 37.4 jit_solution(11974472970225681189)
XLA Ops:
  0.6 0.0 copy-start
  0.6 0.7 %copy-done = f32[1024]{0:T(1024)S(1)} copy-done((f32[1024]{0:T(1024)S(1)}, f32[1024]{0:T(1024)}, u32[]{:S(2)}) %copy-start) | copy-done | bytes 4120
  1.3 0.0 copy-start.1
  1.3 0.7 %copy-done.1 = f32[2,2,256]{2,1,0:T(2,128)S(1)} copy-done((f32[2,2,256]{2,1,0:T(2,128)S(1)}, f32[2,2,256]{2,1,0:T(2,128)}, u32[]{:S(2)}) %copy-start.1) | copy-done | bytes 4120
  2.0 34.2 %shard_map.86 = (bf16[2,48,256]{2,1,0:T(8,128)(2,1)S(1)}, bf16[1,24,256]{2,1,0:T(8,128)(2,1)S(1)}) custom-call(f32[192,512]{1,0:T(8,128)} %tokens_ref.1, f32[1,1024]{1,0:T(1,128)S(1)} %bitcast.2, bf16[3,1024,512]{2,1,0:T(8,128)(2,1)} %qkv_hbm.1, bf16[512,1024]{1,0:T(8,128)(2,1)} %out_hbm.1, bf16[2,1024,256]{2,1,0:T(8,128)(2,1)} %lateral_hbm.1, ...), custom_call_target="tpu_custom_call" | custom-call | tf_op jit(solution)/shard_map/pallas_call | solution.py:461
  36.2 0.6 %copy.11 = bf16[2,48,256]{2,1,0:T(8,128)(2,1)} copy(bf16[2,48,256]{2,1,0:T(8,128)(2,1)S(1)} %get-tuple-element.4) | data formatting | bytes 98304
  36.8 0.6 %copy.12 = bf16[1,24,256]{2,1,0:T(8,128)(2,1)} copy(bf16[1,24,256]{2,1,0:T(8,128)(2,1)S(1)} %get-tuple-element.5) | data formatting | bytes 24576
Async XLA Ops:
  0.6 0.7 %copy-start = (f32[1024]{0:T(1024)S(1)}, f32[1024]{0:T(1024)}, u32[]{:S(2)}) copy-start(f32[1024]{0:T(1024)} %param.8) | copy-start | bytes 12292
  1.3 0.7 %copy-start.1 = (f32[2,2,256]{2,1,0:T(2,128)S(1)}, f32[2,2,256]{2,1,0:T(2,128)}, u32[]{:S(2)}) copy-start(f32[2,2,256]{2,1,0:T(2,128)} %gains_hbm.1) | copy-start | bytes 12292

commit v6 on v4

--- a/solution.py
+++ b/solution.py
@@ -13,7 +13,6 @@
 SUBS = 4
 F32 = jnp.float32
 BF16 = jnp.bfloat16
-NT = (((1,), (1,)), ((), ()))
 
 
 def layer_norm(values_in, gain_row):
@@ -25,10 +24,6 @@
 
 def dot(lhs, rhs):
     return jnp.dot(lhs, rhs, preferred_element_type=F32)
-
-
-def dot_nt(lhs, rhs):
-    return lax.dot_general(lhs, rhs, NT, preferred_element_type=F32)
 
 
 def kernel(
@@ -46,7 +41,6 @@
     half = rows // 2
     cols = GW // 2
     pairs = qbd.shape[0]
-    pair_rows = qbd.shape[1]
 
     even = blk % 2 == 0
     up_ring = jnp.where(
@@ -184,7 +178,7 @@
         scores = []
         for pair in which:
             base = pair * per_pair // quad * quad
-            scores.append(dot_nt(kbuf[:keys, base : base + quad], qbd[pair]))
+            scores.append(dot(kbuf[:keys, base : base + quad], qbd[pair]))
         for pair, score in zip(which, scores):
             before = peak[pair]
             now = jnp.maximum(before, jnp.max(score, axis=0, keepdims=True))
@@ -242,15 +236,17 @@
     weights_in[0].wait()
     queries = (dot(normed[...], qkv[0]) * (HEAD_DIM ** -0.5)).astype(BF16)
     per_pair = 2 * HEAD_DIM
-    quad = qbd.shape[2]
+    quad = qbd.shape[1]
     lane = lax.broadcasted_iota(jnp.int32, (rows, quad), 1)
     for pair in range(pairs):
         base = pair * per_pair // quad * quad
         block = queries[:, base : base + quad]
+        both = []
         for inner in range(2):
             first = pair * per_pair + inner * HEAD_DIM - base
             keep = (lane >= first) & (lane < first + HEAD_DIM)
-            qbd[pair, inner * rows : (inner + 1) * rows, :] = jnp.where(keep, block, jnp.zeros_like(block))
+            both.append(jnp.where(keep, block, jnp.zeros_like(block)))
+        qbd[pair] = jnp.concatenate(both, axis=0).T
     arrive(1, 0)
     weights_in[1].wait()
     keys_of(own_chunk())
@@ -286,10 +282,10 @@
 
     pair_lane = lax.broadcasted_iota(jnp.int32, (rows, per_pair), 1)
     for pair in range(pairs):
-        done = (acc[pair] / total[pair]).T
+        done = (acc[pair] * (1.0 / total[pair])).astype(BF16).T
         att[:, pair * per_pair : (pair + 1) * per_pair] = jnp.where(
             pair_lane < HEAD_DIM, done[:rows], done[rows:]
-        ).astype(BF16)
+        )
 
     weights_in[3].wait()
 
@@ -449,7 +445,7 @@
             pltpu.VMEM((rows, width), BF16),
             pltpu.VMEM((hops, SUBS, rows // SUBS, width), BF16),
             pltpu.VMEM((hops, SUBS, rows // SUBS, width), BF16),
-            pltpu.VMEM((pairs, 2 * rows, quad), BF16),
+            pltpu.VMEM((pairs, quad, 2 * rows), BF16),
             pltpu.VMEM((2 * rows, heads_width), BF16),
             pltpu.VMEM((heads_width, 2 * rows), BF16),
             pltpu.VMEM((pairs, per_pair, 2 * rows), F32),

time: 37.3 us -> 37.2 us (level)
  no operation moved by 1% of the time
where the time goes in v6:
time: 37.2 us; the launch traced here: 37 us
  Pallas kernels  33.7 us (91%)
  local copies, waits for them, and re-layouts  2.59 us (7%)
  between operations  0.65 us (2%)
    pallas_call x1, Pallas kernels, body(): pl.pallas_call(functools.partial(kernel, count), out_shape=(jax.ShapeDtyp...  33.7 us
    unnamed x6, local copies, waits for them, and re-layouts  2.59 us

profile of v6, /device:TPU:9, one launch (start us, length us, event | category | flops | bytes accessed | tf_op | source)
XLA Modules:
  0.0 37.0 jit_solution(4737958423173756976)
XLA Ops:
  0.6 0.0 copy-start
  0.6 0.7 %copy-done = f32[1024]{0:T(1024)S(1)} copy-done((f32[1024]{0:T(1024)S(1)}, f32[1024]{0:T(1024)}, u32[]{:S(2)}) %copy-start) | copy-done | bytes 4120
  1.3 0.0 copy-start.1
  1.3 0.7 %copy-done.1 = f32[2,2,256]{2,1,0:T(2,128)S(1)} copy-done((f32[2,2,256]{2,1,0:T(2,128)S(1)}, f32[2,2,256]{2,1,0:T(2,128)}, u32[]{:S(2)}) %copy-start.1) | copy-done | bytes 4120
  2.0 33.7 %shard_map.86 = (bf16[2,48,256]{2,1,0:T(8,128)(2,1)S(1)}, bf16[1,24,256]{2,1,0:T(8,128)(2,1)S(1)}) custom-call(f32[192,512]{1,0:T(8,128)} %tokens_ref.1, f32[1,1024]{1,0:T(1,128)S(1)} %bitcast.2, bf16[3,1024,512]{2,1,0:T(8,128)(2,1)} %qkv_hbm.1, bf16[512,1024]{1,0:T(8,128)(2,1)} %out_hbm.1, bf16[2,1024,256]{2,1,0:T(8,128)(2,1)} %lateral_hbm.1, ...), custom_call_target="tpu_custom_call" | custom-call | tf_op jit(solution)/shard_map/pallas_call | solution.py:431
  35.8 0.6 %copy.11 = bf16[2,48,256]{2,1,0:T(8,128)(2,1)} copy(bf16[2,48,256]{2,1,0:T(8,128)(2,1)S(1)} %get-tuple-element.4) | data formatting | bytes 98304
  36.4 0.6 %copy.12 = bf16[1,24,256]{2,1,0:T(8,128)(2,1)} copy(bf16[1,24,256]{2,1,0:T(8,128)(2,1)S(1)} %get-tuple-element.5) | data formatting | bytes 24576
Async XLA Ops:
  0.6 0.7 %copy-start = (f32[1024]{0:T(1024)S(1)}, f32[1024]{0:T(1024)}, u32[]{:S(2)}) copy-start(f32[1024]{0:T(1024)} %param.8) | copy-start | bytes 12292
  1.3 0.7 %copy-start.1 = (f32[2,2,256]{2,1,0:T(2,128)S(1)}, f32[2,2,256]{2,1,0:T(2,128)}, u32[]{:S(2)}) copy-start(f32[2,2,256]{2,1,0:T(2,128)} %gains_ref.1) | copy-start | bytes 12292

commit v7 on v6

--- a/solution.py
+++ b/solution.py
@@ -233,6 +233,12 @@
         arrive(step, 3)
         attend(high, keys)
 
+    weights_in[1].wait()
+    keys_of(own_chunk())
+    arrive(1, 0)
+    weights_in[2].wait()
+    values_of(own_chunk())
+    arrive(1, 1)
     weights_in[0].wait()
     queries = (dot(normed[...], qkv[0]) * (HEAD_DIM ** -0.5)).astype(BF16)
     per_pair = 2 * HEAD_DIM
@@ -247,12 +253,6 @@
             keep = (lane >= first) & (lane < first + HEAD_DIM)
             both.append(jnp.where(keep, block, jnp.zeros_like(block)))
         qbd[pair] = jnp.concatenate(both, axis=0).T
-    arrive(1, 0)
-    weights_in[1].wait()
-    keys_of(own_chunk())
-    arrive(1, 1)
-    weights_in[2].wait()
-    values_of(own_chunk())
     arrive(1, 2)
     attend(low, rows)
     arrive(1, 3)

time: 37.2 us -> 37.2 us (level)
  no operation moved by 1% of the time
where the time goes in v7:
time: 37.2 us; the launch traced here: 37 us
  Pallas kernels  33.7 us (91%)
  local copies, waits for them, and re-layouts  2.59 us (7%)
  between operations  0.65 us (2%)
    pallas_call x1, Pallas kernels, body(): pl.pallas_call(functools.partial(kernel, count), out_shape=(jax.ShapeDtyp...  33.7 us
    unnamed x6, local copies, waits for them, and re-layouts  2.59 us

profile of v7, /device:TPU:9, one launch (start us, length us, event | category | flops | bytes accessed | tf_op | source)
XLA Modules:
  0.0 37.0 jit_solution(1502741398188977042)
XLA Ops:
  0.6 0.0 copy-start
  0.6 0.7 %copy-done = f32[1024]{0:T(1024)S(1)} copy-done((f32[1024]{0:T(1024)S(1)}, f32[1024]{0:T(1024)}, u32[]{:S(2)}) %copy-start) | copy-done | bytes 4120
  1.3 0.0 copy-start.1
  1.3 0.7 %copy-done.1 = f32[2,2,256]{2,1,0:T(2,128)S(1)} copy-done((f32[2,2,256]{2,1,0:T(2,128)S(1)}, f32[2,2,256]{2,1,0:T(2,128)}, u32[]{:S(2)}) %copy-start.1) | copy-done | bytes 4120
  2.0 33.7 %shard_map.86 = (bf16[2,48,256]{2,1,0:T(8,128)(2,1)S(1)}, bf16[1,24,256]{2,1,0:T(8,128)(2,1)S(1)}) custom-call(f32[192,512]{1,0:T(8,128)} %tokens_ref.1, f32[1,1024]{1,0:T(1,128)S(1)} %bitcast.2, bf16[3,1024,512]{2,1,0:T(8,128)(2,1)} %qkv_hbm.1, bf16[512,1024]{1,0:T(8,128)(2,1)} %out_hbm.1, bf16[2,1024,256]{2,1,0:T(8,128)(2,1)} %lateral_hbm.1, ...), custom_call_target="tpu_custom_call" | custom-call | tf_op jit(solution)/shard_map/pallas_call | solution.py:431
  35.8 0.6 %copy.11 = bf16[2,48,256]{2,1,0:T(8,128)(2,1)} copy(bf16[2,48,256]{2,1,0:T(8,128)(2,1)S(1)} %get-tuple-element.4) | data formatting | bytes 98304
  36.4 0.6 %copy.12 = bf16[1,24,256]{2,1,0:T(8,128)(2,1)} copy(bf16[1,24,256]{2,1,0:T(8,128)(2,1)S(1)} %get-tuple-element.5) | data formatting | bytes 24576
Async XLA Ops:
  0.6 0.7 %copy-start = (f32[1024]{0:T(1024)S(1)}, f32[1024]{0:T(1024)}, u32[]{:S(2)}) copy-start(f32[1024]{0:T(1024)} %param.8) | copy-start | bytes 12292
  1.3 0.7 %copy-start.1 = (f32[2,2,256]{2,1,0:T(2,128)S(1)}, f32[2,2,256]{2,1,0:T(2,128)}, u32[]{:S(2)}) copy-start(f32[2,2,256]{2,1,0:T(2,128)} %gains_ref.1) | copy-start | bytes 12292
